TPU v7x, 512 devices: a whole 4x8x8 slice. The times are simulated.
512 devices in a mesh: ctx: 64 (over z, x, core), head: 8 (over y).
Axes of the slice: x: 4, y: 8, z: 8, core: 2. Of those that a mesh axis runs over, the one named last changes fastest.
Arguments:
- queries: bfloat16 [16384, 5120], P('ctx', 'head'), may hold values from -6 to 6
- keys: bfloat16 [16384, 5120], P('ctx', 'head'), may hold values from -6 to 6
- values: bfloat16 [16384, 5120], P('ctx', 'head'), may hold values from -21 to 21
- out_grad: bfloat16 [16384, 5120], P('ctx', 'head'), may hold values from -6 to 6
- rates: float32 [40], P('head'), may hold values from 6.1035156e-06 to 0.08
- gain: float32 [5120], P('head'), may hold values from 0.5 to 1.5
Outputs:
- query_grad: bfloat16 [16384, 5120], P('ctx', 'head')
- key_grad: bfloat16 [16384, 5120], P('ctx', 'head')
- value_grad: bfloat16 [16384, 5120], P('ctx', 'head')
All inputs are finite; a program needn't handle non-finite values.
Results may differ from a plain program's by a relative error of at most 0.0069.
Values sent between devices are 32-bit elements; how exact they have to be, the bound alone decides.
No kernel may reach another device: no remote copies, remote signals or barrier semaphores. Data moves between devices by JAX's collectives and lax.ppermute only.
A program may use at most 128 MiB of HBM per device.

v0:
```python
import jax
import jax.numpy as jnp
from jax import lax
from jax.sharding import PartitionSpec as P

HD = 128
HEADS = 40
BLOCK = 256


epsilon = 1e-05


def prefix(value, axis, join, neutral, backward):
    count, mine = (lax.axis_size(axis), lax.axis_index(axis))
    pieces = jax.tree.map(lambda part: lax.all_gather(part, axis), value)
    if backward:
        pieces = jax.tree.map(lambda part: part[::-1], pieces)
        mine = count - 1 - mine
    so_far = jax.tree.map(
        lambda part, zero: jnp.full_like(part, 0) + jnp.asarray(zero, part.dtype), value, neutral
    )

    def turn(position, so_far):
        longer = join(so_far, jax.tree.map(lambda part: part[position], pieces))
        return jax.tree.map(lambda new, old: jnp.where(position < mine, new, old), longer, so_far)

    return lax.fori_loop(0, count - 1, turn, so_far)


def decay_tables(rates):
    places = jnp.arange(BLOCK, dtype=jnp.float32)
    decay_in = jnp.exp(-rates[:, None] * (places[None, :] + 1.0))
    decay_out = jnp.exp(-rates[:, None] * (BLOCK - 1.0 - places)[None, :])
    offsets = places[:, None] - places[None, :]
    decay_mask = jnp.where(
        offsets[None] >= 0.0, jnp.exp(-rates[:, None, None] * jnp.maximum(offsets, 0.0)[None]), 0.0
    )
    block_decay = jnp.exp(-rates * BLOCK)
    return (decay_in, decay_out, decay_mask, block_decay)


def combine(earlier, later):
    return (earlier[0] * later[0], later[0][:, None, None] * earlier[1] + later[1])


def head_major(array, block_count, head_count, head_size):
    return array.reshape(block_count, BLOCK, head_count, head_size).transpose(2, 0, 1, 3)


def token_major(array, tokens_here, width):
    return array.astype(jnp.bfloat16).transpose(1, 2, 0, 3).reshape(tokens_here, width)


def per_device(queries, keys, values, out_grad, rates, gain):
    tokens_here, width = queries.shape
    head_count = rates.shape[0]
    head_size = width // head_count
    block_count = tokens_here // BLOCK
    query_all = head_major(queries, block_count, head_count, head_size)
    key_all = head_major(keys, block_count, head_count, head_size)
    value_all = head_major(values, block_count, head_count, head_size)
    grad_in = head_major(out_grad, block_count, head_count, head_size)
    decay_in, decay_out, decay_mask, block_decay = decay_tables(rates)
    scale_in = decay_in[:, None, :, None]
    scale_out = decay_out[:, None, :, None]
    mask_all = decay_mask[:, None]
    query_dec = (query_all * scale_in).astype(jnp.bfloat16)
    key_dec = (key_all * scale_out).astype(jnp.bfloat16)
    value_dec = (value_all * scale_out).astype(jnp.bfloat16)
    scores = jnp.einsum("hnid,hnjd->hnij", query_all, key_all, preferred_element_type=jnp.float32)
    attn = (scores * mask_all).astype(jnp.bfloat16)
    kv_terms = jnp.einsum("hnid,hnie->hnde", key_dec, value_all, preferred_element_type=jnp.float32)
    decay_col = block_decay[:, None, None]
    local_total = jnp.zeros((head_count, head_size, head_size), jnp.float32)
    block_id = 0
    local_total = decay_col * local_total + kv_terms[:, block_id]
    device_decay = block_decay**block_count
    identity = (jnp.ones_like(device_decay), jnp.zeros_like(local_total))
    incoming = prefix((device_decay, local_total), "ctx", combine, identity, False)[1]
    block_id = 0
    held_list = [incoming.astype(jnp.bfloat16)]
    held_all = jnp.stack(held_list, axis=1)
    attn_out = jnp.einsum("hnij,hnje->hnie", attn, value_all, preferred_element_type=jnp.float32)
    attn_out = attn_out + jnp.einsum(
        "hnid,hnde->hnie", query_dec, held_all, preferred_element_type=jnp.float32
    )
    weighted = grad_in * gain.reshape(head_count, head_size)[:, None, None, :]
    square_sum = jnp.sum(attn_out * attn_out, axis=(0, 3))
    cross_sum = jnp.sum(weighted * attn_out, axis=(0, 3))
    total_square, total_cross = lax.psum((square_sum, cross_sum), "head")
    inverse_norm = lax.rsqrt(total_square / (HEADS * HD) + epsilon)[None, :, :, None]
    d_out = (
        weighted * inverse_norm
        - attn_out * inverse_norm**3 * total_cross[None, :, :, None] / (HEADS * HD)
    ).astype(jnp.bfloat16)
    back_scores = jnp.einsum(
        "hnie,hnje->hnij", d_out, value_all, preferred_element_type=jnp.float32
    )
    back_attn = (back_scores * mask_all).astype(jnp.bfloat16)
    grad_dec = (d_out * scale_in).astype(jnp.bfloat16)
    query_grad = jnp.einsum(
        "hnij,hnjd->hnid", back_attn, key_all, preferred_element_type=jnp.float32
    )
    query_grad = query_grad + jnp.einsum(
        "hnie,hnde->hnid", grad_dec, held_all, preferred_element_type=jnp.float32
    )
    qo_terms = jnp.einsum("hnid,hnie->hnde", query_dec, d_out, preferred_element_type=jnp.float32)
    local_back = jnp.zeros((head_count, head_size, head_size), jnp.float32)
    for block_id in reversed(range(block_count)):
        local_back = decay_col * local_back + qo_terms[:, block_id]
    outgoing = prefix((device_decay, local_back), "ctx", combine, identity, True)[1]
    later_list = [None] * block_count
    running_back = outgoing
    for block_id in reversed(range(block_count)):
        later_list[block_id] = running_back.astype(jnp.bfloat16)
        running_back = decay_col * running_back + qo_terms[:, block_id]
    later_all = jnp.stack(later_list, axis=1)
    key_grad = jnp.einsum(
        "hnij,hnid->hnjd", back_attn, query_all, preferred_element_type=jnp.float32
    )
    key_grad = key_grad + jnp.einsum(
        "hnie,hnde->hnid", value_dec, later_all, preferred_element_type=jnp.float32
    )
    value_grad = jnp.einsum("hnij,hnie->hnje", attn, d_out, preferred_element_type=jnp.float32)
    value_grad = value_grad + jnp.einsum(
        "hnid,hnde->hnie", key_dec, later_all, preferred_element_type=jnp.float32
    )
    return (
        token_major(query_grad, tokens_here, width),
        token_major(key_grad, tokens_here, width),
        token_major(value_grad, tokens_here, width),
    )


def solution(mesh):
    in_specs = (
        P("ctx", "head"),
        P("ctx", "head"),
        P("ctx", "head"),
        P("ctx", "head"),
        P("head"),
        P("head"),
    )
    out_specs = (P("ctx", "head"), P("ctx", "head"), P("ctx", "head"))
    return jax.shard_map(
        per_device, mesh=mesh, in_specs=in_specs, out_specs=out_specs, check_vma=False
    )
```

profile of v0, /device:TPU:1, one launch (start us, length us, event | category | flops | bytes accessed | tf_op | source)
XLA Modules:
  0.0 449.0 jit_solution(15875658513546862518)
XLA Ops:
  7.3 1.2 copy.50
  8.5 1.2 copy.47
  9.7 1.3 dynamic-slice
  12.9 132.5 %all-reduce = f32[320]{0:T(512)S(1)} all-reduce(f32[320]{0:T(512)S(1)} %get-tuple-element.261), channel_id=2, replica_groups=mesh['ctx'=64,'head'=8] {'ctx'}, use_global_device_ids=true, to_apply=%add | all-reduce | flops 320 | bytes 2560
  146.6 70.9 %while.28 = (s32[]{:T(128)}, f32[5,128,128]{2,1,0:T(8,128)S(1)}, s32[]{:T(128)}, f32[64,5]{1,0:T(8,128)S(1)}, f32[64,5,128,128]{3,2,1,0:T(8,128)}, /*index=5*/s32[]{:T(128)}, s32[]{:T(128)}) while((s32[]{:T(128)}, f32[5,128,128]{2,1,0:T(8,128)S(1)}, s32[]{:T(128)}, f32[64,5]{1,0:T(8,128)S(1)}, f32[64,5,128,128]{3,2,1,0:T(8,128)}, ...), condition=%wide.region_1.2_spmd.clone, body=%wide.region_0.1_spmd.clone.sunk | while | flops 327684 | bytes 983205 | solution.py:28
  146.7 1.2 fusion.48
  147.9 1.1 fusion.48
  149.1 1.1 fusion.48
  150.2 1.1 fusion.48
  151.3 1.1 fusion.48
  152.4 1.1 fusion.48
  153.6 1.1 fusion.48
  154.7 1.1 fusion.48
  155.8 1.1 fusion.48
  156.9 1.1 fusion.48
  158.1 1.1 fusion.48
  159.2 1.1 fusion.48
  160.3 1.1 fusion.48
  161.4 1.1 fusion.48
  162.5 1.1 fusion.48
  163.7 1.1 fusion.48
  164.8 1.1 fusion.48
  165.9 1.1 fusion.48
  167.0 1.1 fusion.48
  168.2 1.1 fusion.48
  169.3 1.1 fusion.48
  170.4 1.1 fusion.48
  171.5 1.1 fusion.48
  172.7 1.1 fusion.48
  173.8 1.1 fusion.48
  174.9 1.1 fusion.48
  176.0 1.1 fusion.48
  177.1 1.1 fusion.48
  178.3 1.1 fusion.48
  179.4 1.1 fusion.48
  186.1 1.1 fusion.48
  187.3 1.1 fusion.48
  188.4 1.1 fusion.48
  197.4 1.1 fusion.48
  198.5 1.1 fusion.48
  207.5 1.1 fusion.48
  208.6 1.1 fusion.48
  209.7 1.1 fusion.48
  219.3 14.1 %all-reduce.1 = (f32[256]{0:T(256)S(1)}, f32[1,256]{1,0:T(1,128)S(1)}) all-reduce(f32[256]{0:T(256)} %get-tuple-element.265, f32[1,256]{1,0:T(1,128)S(1)} %bitcast.125), channel_id=1, replica_groups=mesh['ctx'=64,'head'=8] {'head'}, use_global_device_ids=true, to_apply=%region_5.6 | all-reduce | flops 512 | bytes 4096 | tf_op jit(solution)/shard_map/psum | solution.py:91
  237.9 113.7 %all-gather.8.cloned.1.call-done = f32[320,128,128]{2,1,0:T(8,128)} async-done(((f32[5,128,128]{2,1,0:T(8,128)}), f32[320,128,128]{2,1,0:T(8,128)}) %all-gather.8.cloned.1.call-update) | async-done | bytes 20971536 | tf_op jit(solution)/shard_map/all_gather | solution.py:16
  351.5 16.2 %rev.7 = f32[64,5,128,128]{3,2,1,0:T(8,128)} reverse(f32[64,5,128,128]{3,2,1,0:T(8,128)} %bitcast.102), dimensions={0} | reverse | bytes 41943040 | tf_op jit(solution)/shard_map/rev | solution.py:18
  367.7 70.8 %while.29 = (s32[]{:T(128)}, f32[5,128,128]{2,1,0:T(8,128)S(1)}, s32[]{:T(128)}, f32[64,5]{1,0:T(8,128)S(1)}, f32[64,5,128,128]{3,2,1,0:T(8,128)}, /*index=5*/s32[]{:T(128)}, s32[]{:T(128)}) while((s32[]{:T(128)}, f32[5,128,128]{2,1,0:T(8,128)S(1)}, s32[]{:T(128)}, f32[64,5]{1,0:T(8,128)S(1)}, f32[64,5,128,128]{3,2,1,0:T(8,128)}, ...), condition=%wide.region_7.8_spmd.clone, body=%wide.region_6.7_spmd.clone.sunk | while | flops 327684 | bytes 983205 | solution.py:28
  368.8 1.1 fusion.49
  370.0 1.1 fusion.49
  374.5 1.1 fusion.49
  380.1 1.1 fusion.49
  385.7 1.1 fusion.49
  390.2 1.1 fusion.49
  391.3 1.1 fusion.49
  395.8 1.1 fusion.49
  401.4 1.1 fusion.49
  407.1 1.1 fusion.49
  411.5 1.1 fusion.49
  412.7 1.1 fusion.49
  417.2 1.1 fusion.49
  422.8 1.1 fusion.49
  428.4 1.1 fusion.49
  432.9 1.1 fusion.49
  434.0 1.1 fusion.49
  (265 shorter events, 90.2 us)
Async XLA Ops:
  7.2 4.4 copy-start.15
  7.2 139.4 %all-gather.6.cloned.1.call-start = ((), (), s32[]{:S(2)}) async-start(), calls=%async_computation | async-start | bytes 21299200 | tf_op jit(solution)/shard_map/all_gather | solution.py:16
  7.2 138.3 %copy-start.4 = (bf16[256,640]{1,0:T(8,128)(2,1)S(1)}, bf16[256,640]{1,0:T(8,128)(2,1)}, u32[]{:S(2)}) copy-start(bf16[256,640]{1,0:T(8,128)(2,1)} %param.10) | copy-start | bytes 983044
  8.4 137.3 %copy-start.5 = (bf16[256,640]{1,0:T(8,128)(2,1)S(1)}, bf16[256,640]{1,0:T(8,128)(2,1)}, u32[]{:S(2)}) copy-start(bf16[256,640]{1,0:T(8,128)(2,1)} %param.13) | copy-start | bytes 983044
  11.7 1.1 copy-start.11
  11.7 134.4 %copy-start.13 = (f32[5]{0:T(128)}, f32[5]{0:T(128)S(1)}, u32[]{:S(2)}) copy-start(f32[5]{0:T(128)S(1)} %get-tuple-element.262) | copy-start | bytes 64
  12.8 338.7 %all-gather.8.cloned.1.call-start = ((), (), s32[]{:S(2)}) async-start(), calls=%async_computation.1 | async-start | bytes 21299200 | tf_op jit(solution)/shard_map/all_gather | solution.py:16
  146.0 0.6 copy-start.8
  146.6 71.6 %copy-start = (bf16[5,256,256]{2,1,0:T(8,128)(2,1)}, bf16[5,256,256]{2,1,0:T(8,128)(2,1)S(1)}, u32[]{:S(2)}) copy-start(bf16[5,256,256]{2,1,0:T(8,128)(2,1)S(1)} %fusion.2) | copy-start | bytes 1966084
  217.6 0.6 copy-start.6
  217.6 0.7 copy-start.10
  219.2 15.1 %copy-start.12 = (f32[5]{0:T(128)S(1)}, f32[5]{0:T(128)}, u32[]{:S(2)}) copy-start(f32[5]{0:T(128)} %copy-done.11) | copy-start | bytes 64
  233.4 1.9 copy-start.7
  234.3 1.3 copy-start.9
  234.3 1.3 copy-start.14
  236.1 0.8 copy-start.2
  438.5 1.1 copy-start.1
  439.8 1.1 copy-start.3
Sparse Core Ops, SparseCore 0:
  12.9 123.1 all-gather.5
  235.4 116.0 all-gather.7
where the time goes:
time: 454 us; the launch traced here: 449 us
  blocking collectives  147 us (32%)
  other arithmetic  138 us (30%)
  waiting for transfers between devices  114 us (25%)
  local copies, waits for them, and re-layouts  25.9 us (6%)
  between operations  15.1 us (3%)
  matrix products  5.85 us (1%)
    select_n x126, other arithmetic, turn(): jnp.where(position < mine, new, old)  137 us
    unnamed x1, blocking collectives  133 us
    all_gather x2, waiting for transfers between devices, prefix(): pieces = jax.tree.map(lambda part: lax.all_gather(part, axis), value)  114 us
    rev x2, local copies, waits for them, and re-layouts, prefix(): pieces = jax.tree.map(lambda part: part[::-1], pieces)  16.2 us
    psum x1, blocking collectives, per_device(): total_square, total_cross = lax.psum((square_sum, cross_sum), 'head')  14.1 us
  transfers between devices with their start and end apart: 2, of which 1 were waited for; matrix products, arithmetic and copies ran while one was open for 1% of the time, Pallas kernels for 0%

commit v1 on v0

v1 whole, which is shorter than its diff:
```python
import jax
import jax.numpy as jnp
from jax import lax
from jax.experimental import pallas as pl
from jax.experimental.pallas import tpu as pltpu
from jax.sharding import PartitionSpec as P

HD = 128
HEADS = 40
BLOCK = 256
epsilon = 1e-05

F32 = jnp.float32
BF16 = jnp.bfloat16
VMEM = pl.BlockSpec(memory_space=pltpu.VMEM)
SMEM = pl.BlockSpec(memory_space=pltpu.SMEM)


def dot(a, b, ca, cb):
    return lax.dot_general(a, b, (((ca,), (cb,)), ((), ())), preferred_element_type=F32)


def head(ref, h):
    return ref[:, h * HD:(h + 1) * HD]


def decay_in_of(rate):
    place = lax.broadcasted_iota(jnp.int32, (BLOCK, HD), 0).astype(F32)
    return jnp.exp(-rate * (place + 1.0))


def decay_out_of(rate):
    place = lax.broadcasted_iota(jnp.int32, (BLOCK, HD), 0).astype(F32)
    return jnp.exp(-rate * (BLOCK - 1.0 - place))


def mask_of(rate):
    row = lax.broadcasted_iota(jnp.int32, (BLOCK, BLOCK), 0)
    col = lax.broadcasted_iota(jnp.int32, (BLOCK, BLOCK), 1)
    offset = (row - col).astype(F32)
    return jnp.where(offset >= 0.0, jnp.exp(-rate * jnp.maximum(offset, 0.0)), 0.0)


def scaled(ref, h, scale):
    return (head(ref, h).astype(F32) * scale).astype(BF16)


def put_state(ref, h, state):
    halves, chips, width = ref.shape
    share = HD // halves // chips
    for half in range(halves):
        for r in range(share):
            lane = (h * share + r) * HD
            row = half * (HD // halves) + r * chips
            ref[half, :, lane:lane + HD] = state[row:row + chips, :]


def get_state(ref, h):
    halves, chips, width = ref.shape
    share = HD // halves // chips
    rows = []
    for half in range(halves):
        for r in range(share):
            lane = (h * share + r) * HD
            rows.append(ref[half, :, lane:lane + HD])
    return jnp.concatenate(rows, axis=0).astype(BF16)


def kv_kernel(rates, keys, values, terms):
    for h in range(rates.shape[0]):
        key_dec = scaled(keys, h, decay_out_of(rates[h]))
        put_state(terms, h, dot(key_dec, head(values, h), 0, 0))


def intra_kernel(rates, queries, keys, values, attn, intra):
    for h in range(rates.shape[0]):
        scores = dot(head(queries, h), head(keys, h), 1, 1)
        weights = (scores * mask_of(rates[h])).astype(BF16)
        attn[h] = weights
        intra[:, h * HD:(h + 1) * HD] = dot(weights, head(values, h), 1, 0)


def join_kernel(backward, rates, pair, total):
    count = rates.shape[0]
    wide = total.shape[1] // count
    for h in range(count):
        lanes = slice(h * wide, (h + 1) * wide)
        decay = jnp.exp(jnp.full((1, wide), -rates[h] * BLOCK, F32))
        first, second = pair[0, :, lanes], pair[1, :, lanes]
        total[:, lanes] = first + decay * second if backward else decay * first + second


def scan_kernel(backward, rates, totals, prefix):
    count = rates.shape[0]
    chips, width = totals.shape
    wide = width // count
    row = lax.broadcasted_iota(jnp.int32, (chips, chips), 0)
    col = lax.broadcasted_iota(jnp.int32, (chips, chips), 1)
    gap = (col - row - 1) if backward else (row - col - 1)
    far = gap.astype(F32)
    for h in range(count):
        lanes = slice(h * wide, (h + 1) * wide)
        weight = jnp.where(far >= 0.0, jnp.exp(-(rates[h] * (2.0 * BLOCK)) * jnp.maximum(far, 0.0)), 0.0)
        prefix[:, lanes] = lax.dot_general(
            weight, totals[:, lanes], (((1,), (0,)), ((), ())),
            precision=lax.Precision.HIGHEST, preferred_element_type=F32)


def spread_kernel(backward, rates, prefix, pair, states):
    count = rates.shape[0]
    wide = prefix.shape[1] // count
    near, far = (1, 0) if backward else (0, 1)
    for h in range(count):
        lanes = slice(h * wide, (h + 1) * wide)
        decay = jnp.exp(jnp.full((1, wide), -rates[h] * BLOCK, F32))
        incoming = prefix[:, lanes]
        states[near, :, lanes] = incoming
        states[far, :, lanes] = decay * incoming + pair[near, :, lanes]


def out_kernel(rates, queries, out_grad, gain, intra, states, out, held, sums):
    square = jnp.zeros((BLOCK, HD), F32)
    cross = jnp.zeros((BLOCK, HD), F32)
    for h in range(rates.shape[0]):
        lanes = slice(h * HD, (h + 1) * HD)
        state = get_state(states, h)
        held[:, lanes] = state
        query_dec = scaled(queries, h, decay_in_of(rates[h]))
        result = intra[:, lanes] + dot(query_dec, state, 1, 0)
        out[:, lanes] = result
        weighted = head(out_grad, h).astype(F32) * gain[:, lanes]
        square = square + result * result
        cross = cross + weighted * result
    square = jnp.sum(square.T, axis=0, keepdims=True)
    cross = jnp.sum(cross.T, axis=0, keepdims=True)
    both = jnp.concatenate([square, cross], axis=0)
    for peer in range(sums.shape[0]):
        sums[peer] = both


def grad_kernel(rates, queries, out_grad, gain, out, sums, d_out, terms):
    total = jnp.sum(sums[...], axis=0)
    inverse = lax.rsqrt(total[0:1] / (HEADS * HD) + epsilon)
    factor = inverse * inverse * inverse * total[1:2] / (HEADS * HD)
    inverse = jnp.broadcast_to(inverse, (HD, BLOCK)).T
    factor = jnp.broadcast_to(factor, (HD, BLOCK)).T
    for h in range(rates.shape[0]):
        lanes = slice(h * HD, (h + 1) * HD)
        weighted = head(out_grad, h).astype(F32) * gain[:, lanes]
        grad = (weighted * inverse - out[:, lanes] * factor).astype(BF16)
        d_out[:, lanes] = grad
        query_dec = scaled(queries, h, decay_in_of(rates[h]))
        put_state(terms, h, dot(query_dec, grad, 0, 0))


def local_kernel(rates, queries, keys, values, attn, d_out, held, query_grad, key_part, value_part):
    for h in range(rates.shape[0]):
        lanes = slice(h * HD, (h + 1) * HD)
        grad = head(d_out, h)
        back = (dot(grad, head(values, h), 1, 1) * mask_of(rates[h])).astype(BF16)
        grad_dec = (grad.astype(F32) * decay_in_of(rates[h])).astype(BF16)
        query_grad[:, lanes] = (
            dot(back, head(keys, h), 1, 0) + dot(grad_dec, head(held, h), 1, 1)).astype(BF16)
        key_part[:, lanes] = dot(back, head(queries, h), 0, 0)
        value_part[:, lanes] = dot(attn[h], grad, 0, 0)


def last_kernel(rates, keys, values, states, key_part, value_part, key_grad, value_grad):
    for h in range(rates.shape[0]):
        lanes = slice(h * HD, (h + 1) * HD)
        later = get_state(states, h)
        decay_out = decay_out_of(rates[h])
        value_dec = scaled(values, h, decay_out)
        key_dec = scaled(keys, h, decay_out)
        key_grad[:, lanes] = (key_part[:, lanes] + dot(value_dec, later, 1, 1)).astype(BF16)
        value_grad[:, lanes] = (value_part[:, lanes] + dot(key_dec, later, 1, 0)).astype(BF16)


def call(body, name, rates, args, shapes, flops=0):
    outs = [jax.ShapeDtypeStruct(shape, kind) for shape, kind in shapes]
    moved = sum(a.size * a.dtype.itemsize for a in args)
    return pl.pallas_call(
        body,
        out_shape=outs if len(outs) > 1 else outs[0],
        in_specs=[SMEM] + [VMEM] * len(args),
        out_specs=[VMEM] * len(outs) if len(outs) > 1 else VMEM,
        compiler_params=pltpu.CompilerParams(vmem_limit_bytes=24 * 1024 * 1024),
        cost_estimate=pl.CostEstimate(flops=flops, bytes_accessed=moved, transcendentals=0),
        name=name,
    )(rates, *args)


def swap(array, groups):
    return lax.all_to_all(array, "ctx", 0, 0, tiled=True, axis_index_groups=groups)


def scan(terms, rates, chips, backward):
    pairs = [[2 * i, 2 * i + 1] for i in range(chips)]
    rings = [[2 * i + c for i in range(chips)] for c in range(2)]
    width = terms.shape[2]

    def bound(body):
        return lambda *refs: body(backward, *refs)

    pair = swap(terms, pairs)
    total = call(bound(join_kernel), "join", rates, [pair], [((chips, width), F32)])
    total = swap(total, rings)
    prefix = call(bound(scan_kernel), "scan", rates, [total], [((chips, width), F32)])
    prefix = swap(prefix, rings)
    states = call(bound(spread_kernel), "spread", rates, [prefix, pair], [((2, chips, width), F32)])
    return swap(states, pairs)


def per_device(queries, keys, values, out_grad, rates, gain):
    tokens, width = queries.shape
    count = rates.shape[0]
    chips = lax.axis_size("ctx") // 2
    ranks = lax.axis_size("head")
    state_shape = (2, chips, count * HD * HD // 2 // chips)
    gain = gain.reshape(1, width)

    terms = call(kv_kernel, "kv", rates, [keys, values], [(state_shape, F32)])
    attn, intra = call(
        intra_kernel, "intra", rates, [queries, keys, values],
        [((count, BLOCK, BLOCK), BF16), ((BLOCK, width), F32)], 4 * BLOCK * BLOCK * width)
    states = scan(terms, rates, chips, False)
    out, held, sums = call(
        out_kernel, "out", rates, [queries, out_grad, gain, intra, states],
        [((BLOCK, width), F32), ((HD, width), BF16), ((ranks, 2, BLOCK), F32)])
    sums = lax.all_to_all(sums, "head", 0, 0, tiled=True)
    d_out, terms = call(
        grad_kernel, "grad", rates, [queries, out_grad, gain, out, sums],
        [((BLOCK, width), BF16), (state_shape, F32)])
    query_grad, key_part, value_part = call(
        local_kernel, "local", rates, [queries, keys, values, attn, d_out, held],
        [((BLOCK, width), BF16), ((BLOCK, width), F32), ((BLOCK, width), F32)], 8 * BLOCK * BLOCK * width)
    states = scan(terms, rates, chips, True)
    key_grad, value_grad = call(
        last_kernel, "last", rates, [keys, values, states, key_part, value_part],
        [((BLOCK, width), BF16), ((BLOCK, width), BF16)])
    return query_grad, key_grad, value_grad


def solution(mesh):
    spec = P("ctx", "head")
    return jax.shard_map(
        per_device, mesh=mesh, in_specs=(spec, spec, spec, spec, P("head"), P("head")),
        out_specs=(spec, spec, spec), check_vma=False)
```

time: 454 us -> 117 us (0.26)
  other arithmetic: 138 us -> 0 us
  waiting for transfers between devices: 114 us -> 13.6 us
  blocking collectives: 147 us -> 73.4 us
  local copies, waits for them, and re-layouts: 25.9 us -> 7.19 us
  between operations: 15.1 us -> 0.85 us
  Pallas kernels: 0 us -> 12.6 us
  starting transfers between devices: 0.08 us -> 8.48 us
  matrix products: 5.85 us -> 0 us
    select_n x126 -> x0, other arithmetic: 137 us -> none  [turn(): jnp.where(position < mine, new, old)]
    unnamed x1 -> x0, blocking collectives: 133 us -> none
    all_gather x2 -> x0, waiting for transfers between devices: 114 us -> none  [prefix(): pieces = jax.tree.map(lambda part: lax.all_gather(part, axis), value)]
    all_to_all x0 -> x7, blocking collectives: none -> 73.4 us  [the longest x6 60.1 us: swap(): lax.all_to_all(array, 'ctx', 0, 0, tiled=True, axis_index_groups=groups)]
    rev x2 -> x0, local copies, waits for them, and re-layouts: 16.2 us -> none  [prefix(): pieces = jax.tree.map(lambda part: part[::-1], pieces)]
    psum x1 -> x0, blocking collectives: 14.1 us -> none  [per_device(): total_square, total_cross = lax.psum((square_sum, cross_sum), 'head')]
    all_to_all x0 -> x2, waiting for transfers between devices: none -> 13.6 us  [swap(): lax.all_to_all(array, 'ctx', 0, 0, tiled=True, axis_index_groups=groups)]
    pallas_call x0 -> x12, Pallas kernels: none -> 12.6 us  [call(): pl.pallas_call(body, out_shape=outs if len(outs) > 1 else outs[0], in_spe...]
  transfers between devices with their start and end apart: 2 -> 2, of which waited for: 1 -> 2; matrix products, arithmetic and copies ran while one was open for 1% -> 0% of each run, Pallas kernels for 0% -> 4%
where the time goes in v1:
time: 117 us; the launch traced here: 116 us
  blocking collectives  73.4 us (63%)
  waiting for transfers between devices  13.6 us (12%)
  Pallas kernels  12.6 us (11%)
  starting transfers between devices  8.48 us (7%)
  local copies, waits for them, and re-layouts  7.19 us (6%)
    all_to_all x6, blocking collectives, swap(): lax.all_to_all(array, 'ctx', 0, 0, tiled=True, axis_index_groups=groups)  60.1 us
    all_to_all x2, waiting for transfers between devices, swap(): lax.all_to_all(array, 'ctx', 0, 0, tiled=True, axis_index_groups=groups)  13.6 us
    all_to_all x1, blocking collectives, per_device(): sums = lax.all_to_all(sums, 'head', 0, 0, tiled=True)  13.2 us
    pallas_call x12, Pallas kernels, call(): pl.pallas_call(body, out_shape=outs if len(outs) > 1 else outs[0], in_spe...  12.6 us
    all_to_all x2, starting transfers between devices, swap(): lax.all_to_all(array, 'ctx', 0, 0, tiled=True, axis_index_groups=groups)  8.48 us
    unnamed x26, local copies, waits for them, and re-layouts  5.17 us
  transfers between devices with their start and end apart: 2, of which 2 were waited for; matrix products, arithmetic and copies ran while one was open for 0% of the time, Pallas kernels for 4%

profile of v1, /device:TPU:1, one launch (start us, length us, event | category | flops | bytes accessed | tf_op | source)
XLA Modules:
  0.0 116.1 jit_solution(6126431718680761207)
XLA Ops:
  0.6 0.0 copy-start
  0.6 1.0 copy-done
  1.6 0.0 copy-start.2
  1.6 1.0 copy-done.2
  2.6 0.0 copy-start.8
  2.6 0.7 copy-done.8
  3.2 0.9 kv.1
  4.1 10.5 %all_to_all.69.refs_1_.refs_2_ = f32[2,32,1280]{2,1,0:T(8,128)S(1)} all-to-all(f32[2,32,1280]{2,1,0:T(8,128)S(1)} %kv.1), channel_id=1, replica_groups={{0,8},{16,24},{32,40},{48,56},{64,72},{80,88},{96,104},{112,120},{128,1..., dimensions={0} | all-to-all | bytes 655360 | tf_op jit(solution)/shard_map/all_to_all | solution.py:194
  14.6 0.6 join.2
  15.2 0.2 copy.9
  15.4 17.4 %all_to_all.70 = f32[32,1,1280]{2,1,0:T(1,128)S(1)} all-to-all(f32[32,1,1280]{2,1,0:T(1,128)S(1)} %copy.9), channel_id=1, replica_groups={{0,16,32,48,64,80,96,112,128,144,160,176,192,208,224,240,256,272,288,30..., dimensions={0} | all-to-all | bytes 327680 | tf_op jit(solution)/shard_map/all_to_all | solution.py:194
  32.8 0.0 copy-start.10
  32.8 0.0 copy-start.4
  32.8 0.8 scan.2
  33.7 0.0 copy-start.1
  33.7 0.0 copy-start.3
  33.7 0.8 copy.10
  34.5 3.9 %all-to-all-start.2 = ((f32[32,1,1280]{2,1,0:T(1,128)}), f32[32,1,1280]{2,1,0:T(1,128)S(1)}, u32[]{:S(2)}, u32[]{:S(2)}) async-start(f32[32,1,1280]{2,1,0:T(1,128)} %copy.10), calls=%async_computation.2 | async-start | bytes 327680 | tf_op jit(solution)/shard_map/all_to_all | solution.py:194
  38.4 0.0 copy-done.10
  38.4 0.0 copy-start.9
  38.5 0.0 copy-done.4
  38.5 0.0 copy-done.1
  38.5 0.0 copy-done.3
  38.5 0.6 copy-done.9
  39.1 1.3 %intra.1 = (bf16[5,256,256]{2,1,0:T(8,128)(2,1)S(1)}, f32[256,640]{1,0:T(8,128)S(1)}) custom-call(f32[5]{0:T(128)S(1)} %copy-done.9, bf16[256,640]{1,0:T(8,128)(2,1)S(1)} %copy-done.4, bf16[256,640]{1,0:T(8,128)(2,1)S(1)} %copy-done.1, bf16[256,640]{1,0:T(8,128)(2,1)S(1)} %copy-done.3), custom_call_target="tpu_custom_call" | custom-call | flops 167772160 | bytes 983040 | tf_op jit(solution)/shard_map/intra/pallas_call | solution.py:182
  40.4 7.7 %all-to-all-done.2 = f32[32,1,1280]{2,1,0:T(1,128)S(1)} async-done(((f32[32,1,1280]{2,1,0:T(1,128)}), f32[32,1,1280]{2,1,0:T(1,128)S(1)}, u32[]{:S(2)}, u32[]{:S(2)}) %all-to-all-start.2) | async-done | bytes 163872 | tf_op jit(solution)/shard_map/all_to_all | solution.py:194
  48.1 0.6 spread.2
  48.6 0.0 copy-start.5
  48.6 7.0 %all_to_all.71.states = f32[2,32,1280]{2,1,0:T(8,128)S(1)} all-to-all(f32[2,32,1280]{2,1,0:T(8,128)S(1)} %spread.2), channel_id=1, replica_groups={{0,8},{16,24},{32,40},{48,56},{64,72},{80,88},{96,104},{112,120},{128,1..., dimensions={0} | all-to-all | bytes 655360 | tf_op jit(solution)/shard_map/all_to_all | solution.py:194
  55.6 0.0 copy-done.5
  55.6 1.0 out.1
  56.6 13.2 %all_to_all.72.sums = f32[8,2,256]{2,1,0:T(2,128)S(1)} all-to-all(f32[8,2,256]{2,1,0:T(2,128)S(1)} %get-tuple-element.18), channel_id=1, replica_groups=mesh['ctx'=64,'head'=8] {'head'}, dimensions={0} | all-to-all | bytes 32768 | tf_op jit(solution)/shard_map/all_to_all | solution.py:230
  69.9 1.1 grad.1
  70.9 0.0 copy-start.6
  70.9 5.4 %all_to_all.73.refs_1_.refs_2_ = f32[2,32,1280]{2,1,0:T(8,128)S(1)} all-to-all(f32[2,32,1280]{2,1,0:T(8,128)S(1)} %get-tuple-element.22), channel_id=1, replica_groups={{0,8},{16,24},{32,40},{48,56},{64,72},{80,88},{96,104},{112,120},{128,1..., dimensions={0} | all-to-all | bytes 655360 | tf_op jit(solution)/shard_map/all_to_all | solution.py:194
  76.4 0.0 copy-done.6
  76.4 0.6 join.3
  76.9 0.2 copy.11
  77.1 13.1 %all_to_all.74 = f32[32,1,1280]{2,1,0:T(1,128)S(1)} all-to-all(f32[32,1,1280]{2,1,0:T(1,128)S(1)} %copy.11), channel_id=1, replica_groups={{0,16,32,48,64,80,96,112,128,144,160,176,192,208,224,240,256,272,288,30..., dimensions={0} | all-to-all | bytes 327680 | tf_op jit(solution)/shard_map/all_to_all | solution.py:194
  90.3 0.8 scan.3
  91.1 0.8 copy.12
  91.9 4.6 %all-to-all-start.7 = ((f32[32,1,1280]{2,1,0:T(1,128)}), f32[32,1,1280]{2,1,0:T(1,128)}, u32[]{:S(2)}, u32[]{:S(2)}) async-start(f32[32,1,1280]{2,1,0:T(1,128)} %copy.12), calls=%async_computation.7 | async-start | bytes 327680 | tf_op jit(solution)/shard_map/all_to_all | solution.py:194
  96.5 0.0 copy-start.7
  96.5 1.0 copy-done.7
  97.5 2.8 %local.1 = (bf16[256,640]{1,0:T(8,128)(2,1)}, f32[256,640]{1,0:T(8,128)S(1)}, f32[256,640]{1,0:T(8,128)S(1)}) custom-call(f32[5]{0:T(128)S(1)} %copy-done.9, bf16[256,640]{1,0:T(8,128)(2,1)S(1)} %copy-done.4, bf16[256,640]{1,0:T(8,128)(2,1)S(1)} %copy-done.1, bf16[256,640]{1,0:T(8,128)(2,1)S(1)} %copy-done.3, ...), custom_call_target="tpu_custom_call" | custom-call | flops 335544320 | bytes 2129920 | tf_op jit(solution)/shard_map/local/pallas_call | solution.py:182
  100.3 5.9 %all-to-all-done.7 = f32[32,1,1280]{2,1,0:T(1,128)} async-done(((f32[32,1,1280]{2,1,0:T(1,128)}), f32[32,1,1280]{2,1,0:T(1,128)}, u32[]{:S(2)}, u32[]{:S(2)}) %all-to-all-start.7) | async-done | bytes 163872 | tf_op jit(solution)/shard_map/all_to_all | solution.py:194
  106.2 0.9 copy.21
  107.1 0.6 spread.3
  107.7 6.7 %all_to_all.75.states = f32[2,32,1280]{2,1,0:T(8,128)S(1)} all-to-all(f32[2,32,1280]{2,1,0:T(8,128)S(1)} %spread.3), channel_id=1, replica_groups={{0,8},{16,24},{32,40},{48,56},{64,72},{80,88},{96,104},{112,120},{128,1..., dimensions={0} | all-to-all | bytes 655360 | tf_op jit(solution)/shard_map/all_to_all | solution.py:194
  114.4 1.7 %last.1 = (bf16[256,640]{1,0:T(8,128)(2,1)}, bf16[256,640]{1,0:T(8,128)(2,1)}) custom-call(f32[5]{0:T(128)S(1)} %copy-done.9, bf16[256,640]{1,0:T(8,128)(2,1)S(1)} %copy-done.1, bf16[256,640]{1,0:T(8,128)(2,1)S(1)} %copy-done.3, f32[2,32,1280]{2,1,0:T(8,128)S(1)} %all_to_all.75.states, f32[256,640]{1,0:T(8,128)S(1)} %get-tuple-element.23.key_part, ...), custom_call_target="tpu_custom_call" | custom-call | bytes 2293760 | tf_op jit(solution)/shard_map/last/pallas_call | solution.py:182
  (4 shorter events, 0.0 us)
Async XLA Ops:
  0.6 1.0 copy-start
  1.6 1.0 copy-start.2
  2.6 0.7 copy-start.8
  32.8 5.6 %copy-start.10 = (f32[640]{0:T(1024)S(1)}, f32[640]{0:T(1024)}, u32[]{:S(2)}) copy-start(f32[640]{0:T(1024)} %param.11) | copy-start | bytes 7684
  32.8 5.7 %copy-start.4 = (bf16[256,640]{1,0:T(8,128)(2,1)S(1)}, bf16[256,640]{1,0:T(8,128)(2,1)}, u32[]{:S(2)}) copy-start(bf16[256,640]{1,0:T(8,128)(2,1)} %queries.7) | copy-start | bytes 983044
  33.7 4.8 %copy-start.1 = (bf16[256,640]{1,0:T(8,128)(2,1)S(1)}, bf16[256,640]{1,0:T(8,128)(2,1)}, u32[]{:S(2)}) copy-start(bf16[256,640]{1,0:T(8,128)(2,1)} %keys.7) | copy-start | bytes 983044
  33.7 4.8 %copy-start.3 = (bf16[256,640]{1,0:T(8,128)(2,1)S(1)}, bf16[256,640]{1,0:T(8,128)(2,1)}, u32[]{:S(2)}) copy-start(bf16[256,640]{1,0:T(8,128)(2,1)} %values.7) | copy-start | bytes 983044
  34.5 13.5 %all-to-all-start.2 = ((f32[32,1,1280]{2,1,0:T(1,128)}), f32[32,1,1280]{2,1,0:T(1,128)S(1)}, u32[]{:S(2)}, u32[]{:S(2)}) async-start(f32[32,1,1280]{2,1,0:T(1,128)} %copy.10), calls=%async_computation.2 | async-start | bytes 327680 | tf_op jit(solution)/shard_map/all_to_all | solution.py:194
  38.4 0.7 copy-start.9
  48.6 7.0 %copy-start.5 = (bf16[256,640]{1,0:T(8,128)(2,1)S(1)}, bf16[256,640]{1,0:T(8,128)(2,1)}, u32[]{:S(2)}) copy-start(bf16[256,640]{1,0:T(8,128)(2,1)} %out_grad.3) | copy-start | bytes 983044
  70.9 5.4 %copy-start.6 = (bf16[256,640]{1,0:T(8,128)(2,1)}, bf16[256,640]{1,0:T(8,128)(2,1)S(1)}, u32[]{:S(2)}) copy-start(bf16[256,640]{1,0:T(8,128)(2,1)S(1)} %get-tuple-element.19.d_out) | copy-start | bytes 983044
  91.9 14.2 %all-to-all-start.7 = ((f32[32,1,1280]{2,1,0:T(1,128)}), f32[32,1,1280]{2,1,0:T(1,128)}, u32[]{:S(2)}, u32[]{:S(2)}) async-start(f32[32,1,1280]{2,1,0:T(1,128)} %copy.12), calls=%async_computation.7 | async-start | bytes 327680 | tf_op jit(solution)/shard_map/all_to_all | solution.py:194
  96.5 1.0 copy-start.7

commit v2 on v1

v2 whole, which is shorter than its diff:
```python
import functools

import jax
import jax.numpy as jnp
from jax import lax
from jax.experimental import pallas as pl
from jax.experimental.pallas import tpu as pltpu
from jax.sharding import PartitionSpec as P

HD = 128
HEADS = 40
BLOCK = 256
epsilon = 1e-05

F32 = jnp.float32
BF16 = jnp.bfloat16
VMEM = pl.BlockSpec(memory_space=pltpu.VMEM)
HBM = pl.BlockSpec(memory_space=pltpu.HBM)


def dot(a, b, ca, cb):
    return lax.dot_general(a, b, (((ca,), (cb,)), ((), ())), preferred_element_type=F32)


def lanes_of(h):
    return slice(h * HD, (h + 1) * HD)


def head(ref, h):
    return ref[:, lanes_of(h)]


def decay_in_of(rate):
    place = lax.broadcasted_iota(jnp.int32, (BLOCK, HD), 0).astype(F32)
    return jnp.exp(-rate * (place + 1.0))


def decay_out_of(rate):
    place = lax.broadcasted_iota(jnp.int32, (BLOCK, HD), 0).astype(F32)
    return jnp.exp(-rate * (BLOCK - 1.0 - place))


def mask_of(rate):
    row = lax.broadcasted_iota(jnp.int32, (BLOCK, BLOCK), 0)
    col = lax.broadcasted_iota(jnp.int32, (BLOCK, BLOCK), 1)
    offset = (row - col).astype(F32)
    return jnp.where(offset >= 0.0, jnp.exp(-rate * jnp.maximum(offset, 0.0)), 0.0)


def short(rows, h):
    return rows[h:h + 1, 0:HD]


def scaled(array, scale):
    return (array.astype(F32) * scale).astype(BF16)


def put_halves(keep, send, h, state, odd):
    chips = keep.shape[0]
    share = HD // 2 // chips
    low, high = state[:HD // 2], state[HD // 2:]
    mine, other = jnp.where(odd, high, low), jnp.where(odd, low, high)
    for r in range(share):
        lane = (h * share + r) * HD
        keep[:, lane:lane + HD] = mine[r * chips:(r + 1) * chips]
        send[:, lane:lane + HD] = other[r * chips:(r + 1) * chips]


def get_half(ref, h):
    chips = ref.shape[0]
    share = HD // 2 // chips
    return jnp.concatenate([ref[:, lanes_of(h * share + r)] for r in range(share)], axis=0)


def get_state(mine, other, h, odd):
    mine, other = get_half(mine, h), get_half(other, h)
    low, high = jnp.where(odd, other, mine), jnp.where(odd, mine, other)
    return jnp.concatenate([low, high], axis=0).astype(BF16)


def kv_kernel(rates, keys, values, keep, send, rows, mixing, rate, key_in, value_in, sems):
    count = rates.shape[0]
    odd = lax.rem(lax.axis_index("ctx"), 2) == 1
    copies = [pltpu.make_async_copy(rates, rate, sems.at[2 * count])]
    for h in range(count):
        for which, (source, target) in enumerate(((keys, key_in), (values, value_in))):
            copies.append(pltpu.make_async_copy(
                source.at[:, lanes_of(h)], target.at[:, lanes_of(h)], sems.at[2 * h + which]))
    for copy in copies:
        copy.start()
    copies[0].wait()
    wide = mixing.shape[1] // count
    first_rows = lax.broadcasted_iota(jnp.int32, (8, wide), 0)
    for h in range(count):
        rows[h:h + 1, :] = jnp.full((1, BLOCK), rate[h], F32)
        decay = jnp.exp(jnp.full((8, wide), -rate[h] * BLOCK, F32))
        place = lax.rem(first_rows, 4)
        later = first_rows >= 4
        first = later == odd
        on_first = jnp.where(place == 0, decay, jnp.where(place == 2, 0.0, 1.0))
        on_second = jnp.where(place == 1, decay, jnp.where(place == 3, 0.0, 1.0))
        mixing[:, h * wide:(h + 1) * wide] = jnp.where(first, on_first, on_second)
    for h in range(count):
        decay_out = decay_out_of(rate[h])
        copies[1 + 2 * h].wait()
        copies[2 + 2 * h].wait()
        key_dec = scaled(head(key_in, h), decay_out)
        put_halves(keep, send, h, dot(key_dec, head(value_in, h), 0, 0), odd)


def odd_of(mixing):
    return mixing[2:3, 0:HD] > 0.5


def intra_kernel(rows, queries, keys, values, attn, intra):
    for h in range(queries.shape[1] // HD):
        scores = dot(head(queries, h), head(keys, h), 1, 1)
        weights = (scores * mask_of(rows[h:h + 1, :])).astype(BF16)
        attn[h] = weights
        intra[:, lanes_of(h)] = dot(weights, head(values, h), 1, 0)


def scan_kernel(backward, rows, totals, prefix):
    chips, width = totals.shape
    count = width * chips * 2 // HD // HD
    wide = width // count
    row = lax.broadcasted_iota(jnp.int32, (chips, chips), 0)
    col = lax.broadcasted_iota(jnp.int32, (chips, chips), 1)
    far = ((col - row - 1) if backward else (row - col - 1)).astype(F32)
    for h in range(count):
        lanes = slice(h * wide, (h + 1) * wide)
        rate = rows[h:h + 1, 0:chips]
        weight = jnp.where(far >= 0.0, jnp.exp(-(rate * (2.0 * BLOCK)) * jnp.maximum(far, 0.0)), 0.0)
        prefix[:, lanes] = lax.dot_general(
            weight, totals[:, lanes], (((1,), (0,)), ((), ())),
            precision=lax.Precision.HIGHEST, preferred_element_type=F32)


def out_kernel(rows, mixing, queries, out_grad, gain, intra, mine, other, out, held, sums):
    odd = odd_of(mixing)
    square = jnp.zeros((BLOCK, HD), F32)
    cross = jnp.zeros((BLOCK, HD), F32)
    for h in range(queries.shape[1] // HD):
        state = get_state(mine, other, h, odd)
        held[:, lanes_of(h)] = state
        query_dec = scaled(head(queries, h), decay_in_of(short(rows, h)))
        result = head(intra, h) + dot(query_dec, state, 1, 0)
        out[:, lanes_of(h)] = result
        weighted = head(out_grad, h).astype(F32) * head(gain, h)
        square = square + result * result
        cross = cross + weighted * result
    square = jnp.sum(square.T, axis=0, keepdims=True)
    cross = jnp.sum(cross.T, axis=0, keepdims=True)
    both = jnp.concatenate([square, cross], axis=0)
    for peer in range(sums.shape[0]):
        sums[peer] = both


def grad_kernel(rows, mixing, queries, out_grad, gain, out, sums, d_out, keep, send):
    odd = odd_of(mixing)
    total = jnp.sum(sums[...], axis=0)
    inverse = lax.rsqrt(total[0:1] / (HEADS * HD) + epsilon)
    factor = inverse * inverse * inverse * total[1:2] / (HEADS * HD)
    inverse = jnp.broadcast_to(inverse, (HD, BLOCK)).T
    factor = jnp.broadcast_to(factor, (HD, BLOCK)).T
    for h in range(queries.shape[1] // HD):
        weighted = head(out_grad, h).astype(F32) * head(gain, h)
        grad = (weighted * inverse - head(out, h) * factor).astype(BF16)
        d_out[:, lanes_of(h)] = grad
        query_dec = scaled(head(queries, h), decay_in_of(short(rows, h)))
        put_halves(keep, send, h, dot(query_dec, grad, 0, 0), odd)


def local_kernel(rows, queries, keys, values, d_out, held, query_grad, key_part):
    for h in range(queries.shape[1] // HD):
        grad = head(d_out, h)
        back = (dot(grad, head(values, h), 1, 1) * mask_of(rows[h:h + 1, :])).astype(BF16)
        grad_dec = scaled(grad, decay_in_of(short(rows, h)))
        query_grad[:, lanes_of(h)] = (
            dot(back, head(keys, h), 1, 0) + dot(grad_dec, head(held, h), 1, 1)).astype(BF16)
        key_part[:, lanes_of(h)] = dot(back, head(queries, h), 0, 0)


def value_kernel(attn, d_out, value_part):
    for h in range(attn.shape[0]):
        value_part[:, lanes_of(h)] = dot(attn[h], head(d_out, h), 0, 0)


def last_kernel(rows, mixing, keys, values, mine, other, key_part, value_part, key_grad, value_grad):
    odd = odd_of(mixing)
    for h in range(keys.shape[1] // HD):
        later = get_state(mine, other, h, odd)
        decay_out = decay_out_of(short(rows, h))
        value_dec = scaled(head(values, h), decay_out)
        key_dec = scaled(head(keys, h), decay_out)
        key_grad[:, lanes_of(h)] = (head(key_part, h) + dot(value_dec, later, 1, 1)).astype(BF16)
        value_grad[:, lanes_of(h)] = (head(value_part, h) + dot(key_dec, later, 1, 0)).astype(BF16)


def call(body, name, args, shapes, specs=None, scratch=(), flops=0):
    outs = [jax.ShapeDtypeStruct(shape, kind) for shape, kind in shapes]
    moved = sum(a.size * a.dtype.itemsize for a in args)
    return pl.pallas_call(
        body,
        out_shape=outs if len(outs) > 1 else outs[0],
        in_specs=specs or [VMEM] * len(args),
        out_specs=[VMEM] * len(outs) if len(outs) > 1 else VMEM,
        scratch_shapes=list(scratch),
        compiler_params=pltpu.CompilerParams(vmem_limit_bytes=16 * 1024 * 1024),
        cost_estimate=pl.CostEstimate(flops=flops, bytes_accessed=moved, transcendentals=0),
        name=name,
    )(*args)


def scan(keep, send, rows, mixing, beside_first, beside_last, backward):
    chips, width = keep.shape
    partners = [(i, i ^ 1) for i in range(2 * chips)]
    rings = [[2 * i + c for i in range(chips)] for c in range(2)]
    own, coming, add_mine, add_other = (mixing[4 * backward + i][None] for i in range(4))

    got = lax.ppermute(send, "ctx", partners)
    beside_first = beside_first()
    got, beside_first = lax.optimization_barrier((got, beside_first))
    total = own * keep + coming * got
    total = lax.all_to_all(total, "ctx", 0, 0, tiled=True, axis_index_groups=rings)
    prefix = call(functools.partial(scan_kernel, backward), "scan", [rows, total], [((chips, width), F32)])
    prefix = lax.all_to_all(prefix, "ctx", 0, 0, tiled=True, axis_index_groups=rings)
    other = lax.ppermute(own * prefix + add_other * keep, "ctx", partners)
    mine = coming * prefix + add_mine * got
    beside_last = beside_last()
    other, beside_last = lax.optimization_barrier((other, beside_last))
    return mine, other, beside_first, beside_last


def per_device(queries, keys, values, out_grad, rates, gain):
    tokens, width = queries.shape
    count = rates.shape[0]
    chips = lax.axis_size("ctx") // 2
    ranks = lax.axis_size("head")
    half = ((chips, count * HD * HD // 2 // chips), F32)
    gain = gain.reshape(1, width)
    wide16, wide32 = ((BLOCK, width), BF16), ((BLOCK, width), F32)

    keep, send, rows, mixing = call(
        kv_kernel, "kv", [pltpu.with_memory_space_constraint(a, pltpu.HBM) for a in (rates, keys, values)],
        [half, half, ((8, BLOCK), F32), ((8, half[0][1]), F32)],
        specs=[HBM] * 3,
        scratch=[pltpu.SMEM((count,), F32), pltpu.VMEM((BLOCK, width), BF16), pltpu.VMEM((BLOCK, width), BF16),
                 pltpu.SemaphoreType.DMA((2 * count + 1,))])
    mine, other, (attn, intra), unused = scan(
        keep, send, rows, mixing,
        lambda: call(intra_kernel, "intra", [rows, queries, keys, values],
                     [((count, BLOCK, BLOCK), BF16), wide32], flops=4 * BLOCK * BLOCK * width),
        lambda: (), False)
    out, held, sums = call(
        out_kernel, "out", [rows, mixing, queries, out_grad, gain, intra, mine, other],
        [wide32, ((HD, width), BF16), ((ranks, 2, BLOCK), F32)])
    sums = lax.all_to_all(sums, "head", 0, 0, tiled=True)
    d_out, keep, send = call(
        grad_kernel, "grad", [rows, mixing, queries, out_grad, gain, out, sums], [wide16, half, half])
    mine, other, (query_grad, key_part), value_part = scan(
        keep, send, rows, mixing,
        lambda: call(local_kernel, "local", [rows, queries, keys, values, d_out, held], [wide16, wide32],
                     flops=6 * BLOCK * BLOCK * width),
        lambda: call(value_kernel, "value", [attn, d_out], [wide32], flops=2 * BLOCK * BLOCK * width),
        True)
    key_grad, value_grad = call(
        last_kernel, "last", [rows, mixing, keys, values, mine, other, key_part, value_part], [wide16, wide16])
    return query_grad, key_grad, value_grad


def solution(mesh):
    spec = P("ctx", "head")
    return jax.shard_map(
        per_device, mesh=mesh, in_specs=(spec, spec, spec, spec, P("head"), P("head")),
        out_specs=(spec, spec, spec), check_vma=False)
```

time: 117 us -> 105 us (0.90)
  starting transfers between devices: 8.48 us -> 21.8 us
  waiting for transfers between devices: 13.6 us -> 1.6 us
  local copies, waits for them, and re-layouts: 7.19 us -> 1.8 us
  Pallas kernels: 12.6 us -> 7.93 us
  blocking collectives: 73.4 us -> 70.8 us
    ppermute x0 -> x4, starting transfers between devices: none -> 21.8 us  [the longest x2 12.5 us: scan(): got = lax.ppermute(send, 'ctx', partners)]
    all_to_all x2 -> x0, waiting for transfers between devices: 13.6 us -> none  [swap(): lax.all_to_all(array, 'ctx', 0, 0, tiled=True, axis_index_groups=groups)]
    all_to_all x2 -> x0, starting transfers between devices: 8.48 us -> none  [swap(): lax.all_to_all(array, 'ctx', 0, 0, tiled=True, axis_index_groups=groups)]
    pallas_call x12 -> x9, Pallas kernels: 12.6 us -> 7.93 us  [call(): pl.pallas_call(body, out_shape=outs if len(outs) > 1 else outs[0], in_spe...]
    unnamed x26 -> x14, local copies, waits for them, and re-layouts: 5.17 us -> 1.01 us
    all_to_all x6 -> x4, blocking collectives: 60.1 us -> 57.5 us  [the longest x2 30.7 us: scan(): lax.all_to_all(total, 'ctx', 0, 0, tiled=True, axis_index_groups=rings)]
    ppermute x0 -> x4, waiting for transfers between devices: none -> 1.6 us  [the longest x2 1.6 us: scan(): other = lax.ppermute(own * prefix + add_other * keep, 'ctx', partners)]
    all_to_all x4, local copies, waits for them, and re-layouts: 2.02 us -> 0.68 us  [the longest x2 0.34 us: scan(): lax.all_to_all(total, 'ctx', 0, 0, tiled=True, axis_index_groups=rings)]
  transfers between devices with their start and end apart: 2 -> 4, of which waited for: 2 -> 2; matrix products, arithmetic and copies ran while one was open for 0% -> 0% of each run, Pallas kernels for 4% -> 3%
where the time goes in v2:
time: 105 us
  blocking collectives  70.8 us (67%)
  starting transfers between devices  21.8 us (21%)
  Pallas kernels  7.93 us (8%)
  local copies, waits for them, and re-layouts  1.8 us (2%)
  waiting for transfers between devices  1.6 us (2%)
    all_to_all x2, blocking collectives, scan(): lax.all_to_all(total, 'ctx', 0, 0, tiled=True, axis_index_groups=rings)  30.7 us
    all_to_all x2, blocking collectives, scan(): lax.all_to_all(prefix, 'ctx', 0, 0, tiled=True, axis_index_groups=rings)  26.8 us
    all_to_all x1, blocking collectives, per_device(): sums = lax.all_to_all(sums, 'head', 0, 0, tiled=True)  13.2 us
    ppermute x2, starting transfers between devices, scan(): got = lax.ppermute(send, 'ctx', partners)  12.5 us
    ppermute x2, starting transfers between devices, scan(): other = lax.ppermute(own * prefix + add_other * keep, 'ctx', partners)  9.27 us
    pallas_call x9, Pallas kernels, call(): pl.pallas_call(body, out_shape=outs if len(outs) > 1 else outs[0], in_spe...  7.93 us
  transfers between devices with their start and end apart: 4, of which 2 were waited for; matrix products, arithmetic and copies ran while one was open for 0% of the time, Pallas kernels for 3%

profile of v2, /device:TPU:1, one launch (start us, length us, event | category | flops | bytes accessed | tf_op | source)
XLA Modules:
  0.0 104.8 jit_solution(4078042916958484875)
XLA Ops:
  0.6 0.0 copy-start.1
  0.6 0.0 copy-start
  0.7 2.1 %kv.1 = (f32[32,1280]{1,0:T(8,128)S(1)}, f32[32,1280]{1,0:T(8,128)S(1)}, f32[8,256]{1,0:T(8,128)S(1)}, f32[8,1280]{1,0:T(8,128)S(1)}) custom-call(f32[5]{0:T(128)} %rates.1, bf16[256,640]{1,0:T(8,128)(2,1)} %keys.7, bf16[256,640]{1,0:T(8,128)(2,1)} %values.7), custom_call_target="tpu_custom_call" | custom-call | bytes 655380 | tf_op jit(solution)/shard_map/kv/pallas_call | solution.py:203
  2.8 8.8 %collective-permute-start = (f32[32,1280]{1,0:T(8,128)S(1)}, f32[32,1280]{1,0:T(8,128)S(1)}, u32[]{:S(2)}, u32[]{:S(2)}) collective-permute-start(f32[32,1280]{1,0:T(8,128)S(1)} %get-tuple-element.29), channel_id=1, source_target_pairs={{0,8},{8,0},{16,24},{24,16},{32,40},{40,32},{48,56},{56,48},{64,72... | collective-permute-start | bytes 491528 | tf_op jit(solution)/shard_map/ppermute | solution.py:221
  11.6 0.0 copy-done.1
  11.6 0.0 copy-done
  11.6 0.0 copy-start.2
  11.6 1.0 copy-done.2
  12.6 0.7 intra.1
  13.3 0.1 slice_reduce_fusion
  13.4 0.0 collective-permute-done
  13.5 0.2 copy.9
  13.7 17.5 %all_to_all.51 = f32[32,1,1280]{2,1,0:T(1,128)S(1)} all-to-all(f32[32,1,1280]{2,1,0:T(1,128)S(1)} %copy.9), channel_id=1, replica_groups={{0,16,32,48,64,80,96,112,128,144,160,176,192,208,224,240,256,272,288,30..., dimensions={0} | all-to-all | bytes 327680 | tf_op jit(solution)/shard_map/all_to_all | solution.py:225
  31.2 0.3 scan.2
  31.5 0.2 copy.10
  31.6 13.4 %all_to_all.52 = f32[32,1,1280]{2,1,0:T(1,128)S(1)} all-to-all(f32[32,1,1280]{2,1,0:T(1,128)S(1)} %copy.10), channel_id=1, replica_groups={{0,16,32,48,64,80,96,112,128,144,160,176,192,208,224,240,256,272,288,30..., dimensions={0} | all-to-all | bytes 327680 | tf_op jit(solution)/shard_map/all_to_all | solution.py:227
  45.1 0.0 copy-start.5
  45.1 0.0 copy-start.4
  45.1 4.7 %collective-permute-start.1 = (f32[32,1280]{1,0:T(8,128)S(1)}, f32[32,1280]{1,0:T(8,128)S(1)}, u32[]{:S(2)}, u32[]{:S(2)}) collective-permute-start(f32[32,1280]{1,0:T(8,128)S(1)} %get-tuple-element.61), channel_id=1, source_target_pairs={{0,8},{8,0},{16,24},{24,16},{32,40},{40,32},{48,56},{56,48},{64,72... | collective-permute-start | bytes 491528 | tf_op jit(solution)/shard_map/ppermute | solution.py:228
  49.8 0.0 copy-done.5
  49.8 1.0 collective-permute-done.1.other
  50.8 0.0 copy-done.4
  50.8 0.4 out.1
  51.3 13.2 %all_to_all.53.sums = f32[8,2,256]{2,1,0:T(2,128)S(1)} all-to-all(f32[8,2,256]{2,1,0:T(2,128)S(1)} %get-tuple-element.36), channel_id=1, replica_groups=mesh['ctx'=64,'head'=8] {'head'}, dimensions={0} | all-to-all | bytes 32768 | tf_op jit(solution)/shard_map/all_to_all | solution.py:258
  64.5 0.0 copy-start.3
  64.5 0.5 grad.1
  65.0 3.7 %collective-permute-start.2 = (f32[32,1280]{1,0:T(8,128)S(1)}, f32[32,1280]{1,0:T(8,128)S(1)}, u32[]{:S(2)}, u32[]{:S(2)}) collective-permute-start(f32[32,1280]{1,0:T(8,128)S(1)} %get-tuple-element.37), channel_id=1, source_target_pairs={{0,8},{8,0},{16,24},{24,16},{32,40},{40,32},{48,56},{56,48},{64,72... | collective-permute-start | bytes 491528 | tf_op jit(solution)/shard_map/ppermute | solution.py:221
  68.7 0.0 copy-done.3
  68.8 1.9 %local.1 = (bf16[256,640]{1,0:T(8,128)(2,1)}, f32[256,640]{1,0:T(8,128)S(1)}) custom-call(f32[8,256]{1,0:T(8,128)S(1)} %get-tuple-element.27.rows, bf16[256,640]{1,0:T(8,128)(2,1)S(1)} %copy-done, bf16[256,640]{1,0:T(8,128)(2,1)S(1)} %copy-done.1, bf16[256,640]{1,0:T(8,128)(2,1)S(1)} %copy-done.3, bf16[256,640]{1,0:T(8,128)(2,1)S(1)} %get-tuple-element.38.d_out, ...), custom_call_target="tpu_custom_call" | custom-call | flops 251658240 | bytes 1482752 | tf_op jit(solution)/shard_map/local/pallas_call | solution.py:203
  70.7 0.0 collective-permute-done.2
  70.7 0.2 copy.11
  70.9 13.2 %all_to_all.54 = f32[32,1,1280]{2,1,0:T(1,128)S(1)} all-to-all(f32[32,1,1280]{2,1,0:T(1,128)S(1)} %copy.11), channel_id=1, replica_groups={{0,16,32,48,64,80,96,112,128,144,160,176,192,208,224,240,256,272,288,30..., dimensions={0} | all-to-all | bytes 327680 | tf_op jit(solution)/shard_map/all_to_all | solution.py:225
  84.1 0.3 scan.3
  84.4 0.2 copy.12
  84.6 13.4 %all_to_all.55 = f32[32,1,1280]{2,1,0:T(1,128)S(1)} all-to-all(f32[32,1,1280]{2,1,0:T(1,128)S(1)} %copy.12), channel_id=1, replica_groups={{0,16,32,48,64,80,96,112,128,144,160,176,192,208,224,240,256,272,288,30..., dimensions={0} | all-to-all | bytes 327680 | tf_op jit(solution)/shard_map/all_to_all | solution.py:227
  98.0 4.6 %collective-permute-start.3 = (f32[32,1280]{1,0:T(8,128)S(1)}, f32[32,1280]{1,0:T(8,128)S(1)}, u32[]{:S(2)}, u32[]{:S(2)}) collective-permute-start(f32[32,1280]{1,0:T(8,128)S(1)} %get-tuple-element.59), channel_id=1, source_target_pairs={{0,8},{8,0},{16,24},{24,16},{32,40},{40,32},{48,56},{56,48},{64,72... | collective-permute-start | bytes 491528 | tf_op jit(solution)/shard_map/ppermute | solution.py:228
  102.6 0.4 value.1.value_part
  103.0 0.6 collective-permute-done.3.other
  103.6 1.2 %last.1 = (bf16[256,640]{1,0:T(8,128)(2,1)}, bf16[256,640]{1,0:T(8,128)(2,1)}) custom-call(f32[8,256]{1,0:T(8,128)S(1)} %get-tuple-element.27.rows, f32[8,1280]{1,0:T(8,128)S(1)} %get-tuple-element.28.mixing, bf16[256,640]{1,0:T(8,128)(2,1)S(1)} %copy-done.1, bf16[256,640]{1,0:T(8,128)(2,1)S(1)} %copy-done.3, f32[32,1280]{1,0:T(8,128)S(1)} %get-tuple-element.60.mine, ...), custom_call_target="tpu_custom_call" | custom-call | bytes 2342912 | tf_op jit(solution)/shard_map/last/pallas_call | solution.py:203
  (7 shorter events, 0.2 us)
Async XLA Ops:
  0.6 10.9 %copy-start.1 = (bf16[256,640]{1,0:T(8,128)(2,1)S(1)}, bf16[256,640]{1,0:T(8,128)(2,1)}, u32[]{:S(2)}) copy-start(bf16[256,640]{1,0:T(8,128)(2,1)} %keys.7) | copy-start | bytes 983044
  0.6 10.9 %copy-start = (bf16[256,640]{1,0:T(8,128)(2,1)S(1)}, bf16[256,640]{1,0:T(8,128)(2,1)}, u32[]{:S(2)}) copy-start(bf16[256,640]{1,0:T(8,128)(2,1)} %queries.7) | copy-start | bytes 983044
  2.8 10.7 %collective-permute-start = (f32[32,1280]{1,0:T(8,128)S(1)}, f32[32,1280]{1,0:T(8,128)S(1)}, u32[]{:S(2)}, u32[]{:S(2)}) collective-permute-start(f32[32,1280]{1,0:T(8,128)S(1)} %get-tuple-element.29), channel_id=1, source_target_pairs={{0,8},{8,0},{16,24},{24,16},{32,40},{40,32},{48,56},{56,48},{64,72... | collective-permute-start | bytes 491528 | tf_op jit(solution)/shard_map/ppermute | solution.py:221
  11.6 1.0 copy-start.2
  45.1 4.7 %copy-start.5 = (f32[640]{0:T(1024)S(1)}, f32[640]{0:T(1024)}, u32[]{:S(2)}) copy-start(f32[640]{0:T(1024)} %param.11) | copy-start | bytes 7684
  45.1 5.7 %copy-start.4 = (bf16[256,640]{1,0:T(8,128)(2,1)S(1)}, bf16[256,640]{1,0:T(8,128)(2,1)}, u32[]{:S(2)}) copy-start(bf16[256,640]{1,0:T(8,128)(2,1)} %out_grad.3) | copy-start | bytes 983044
  45.1 5.7 %collective-permute-start.1 = (f32[32,1280]{1,0:T(8,128)S(1)}, f32[32,1280]{1,0:T(8,128)S(1)}, u32[]{:S(2)}, u32[]{:S(2)}) collective-permute-start(f32[32,1280]{1,0:T(8,128)S(1)} %get-tuple-element.61), channel_id=1, source_target_pairs={{0,8},{8,0},{16,24},{24,16},{32,40},{40,32},{48,56},{56,48},{64,72... | collective-permute-start | bytes 491528 | tf_op jit(solution)/shard_map/ppermute | solution.py:228
  64.5 4.2 %copy-start.3 = (bf16[256,640]{1,0:T(8,128)(2,1)S(1)}, bf16[256,640]{1,0:T(8,128)(2,1)}, u32[]{:S(2)}) copy-start(bf16[256,640]{1,0:T(8,128)(2,1)} %values.7) | copy-start | bytes 983044
  65.0 5.6 %collective-permute-start.2 = (f32[32,1280]{1,0:T(8,128)S(1)}, f32[32,1280]{1,0:T(8,128)S(1)}, u32[]{:S(2)}, u32[]{:S(2)}) collective-permute-start(f32[32,1280]{1,0:T(8,128)S(1)} %get-tuple-element.37), channel_id=1, source_target_pairs={{0,8},{8,0},{16,24},{24,16},{32,40},{40,32},{48,56},{56,48},{64,72... | collective-permute-start | bytes 491528 | tf_op jit(solution)/shard_map/ppermute | solution.py:221
  98.0 5.6 %collective-permute-start.3 = (f32[32,1280]{1,0:T(8,128)S(1)}, f32[32,1280]{1,0:T(8,128)S(1)}, u32[]{:S(2)}, u32[]{:S(2)}) collective-permute-start(f32[32,1280]{1,0:T(8,128)S(1)} %get-tuple-element.59), channel_id=1, source_target_pairs={{0,8},{8,0},{16,24},{24,16},{32,40},{40,32},{48,56},{56,48},{64,72... | collective-permute-start | bytes 491528 | tf_op jit(solution)/shard_map/ppermute | solution.py:228

commit v3 on v2

--- a/solution.py
+++ b/solution.py
@@ -31,20 +31,30 @@
 
 
 def decay_in_of(rate):
-    place = lax.broadcasted_iota(jnp.int32, (BLOCK, HD), 0).astype(F32)
-    return jnp.exp(-rate * (place + 1.0))
+    place = lax.broadcasted_iota(jnp.int32, (8, HD), 0).astype(F32)
+    table = jnp.exp(-rate * (place + 1.0))
+    while table.shape[0] < BLOCK:
+        step = jnp.exp(jnp.full((1, HD), -float(table.shape[0]), F32) * rate)
+        table = jnp.concatenate([table, table * step], axis=0)
+    return table
 
 
 def decay_out_of(rate):
-    place = lax.broadcasted_iota(jnp.int32, (BLOCK, HD), 0).astype(F32)
-    return jnp.exp(-rate * (BLOCK - 1.0 - place))
-
-
-def mask_of(rate):
+    place = lax.broadcasted_iota(jnp.int32, (8, HD), 0).astype(F32)
+    table = jnp.exp(-rate * (7.0 - place))
+    while table.shape[0] < BLOCK:
+        step = jnp.exp(jnp.full((1, HD), -float(table.shape[0]), F32) * rate)
+        table = jnp.concatenate([table * step, table], axis=0)
+    return table
+
+
+def mask_of(rates, decay_in):
     row = lax.broadcasted_iota(jnp.int32, (BLOCK, BLOCK), 0)
     col = lax.broadcasted_iota(jnp.int32, (BLOCK, BLOCK), 1)
-    offset = (row - col).astype(F32)
-    return jnp.where(offset >= 0.0, jnp.exp(-rate * jnp.maximum(offset, 0.0)), 0.0)
+    place = lax.broadcasted_iota(jnp.int32, (1, BLOCK), 1).astype(F32)
+    growth = jnp.exp(rates * (place + 1.0))
+    both = jnp.concatenate([decay_in, decay_in], axis=1) * growth
+    return jnp.where(row >= col, both, 0.0)
 
 
 def short(rows, h):
@@ -78,7 +88,7 @@
     return jnp.concatenate([low, high], axis=0).astype(BF16)
 
 
-def kv_kernel(rates, keys, values, keep, send, rows, mixing, rate, key_in, value_in, sems):
+def kv_kernel(rates, keys, values, keep, send, rows, mixing, rate, key_in, value_in, decays, sems):
     count = rates.shape[0]
     odd = lax.rem(lax.axis_index("ctx"), 2) == 1
     copies = [pltpu.make_async_copy(rates, rate, sems.at[2 * count])]
@@ -90,21 +100,21 @@
         copy.start()
     copies[0].wait()
     wide = mixing.shape[1] // count
-    first_rows = lax.broadcasted_iota(jnp.int32, (8, wide), 0)
+    index = lax.broadcasted_iota(jnp.int32, (8, wide), 0)
     for h in range(count):
         rows[h:h + 1, :] = jnp.full((1, BLOCK), rate[h], F32)
         decay = jnp.exp(jnp.full((8, wide), -rate[h] * BLOCK, F32))
-        place = lax.rem(first_rows, 4)
-        later = first_rows >= 4
+        place = lax.rem(index, 4)
+        later = index >= 4
         first = later == odd
         on_first = jnp.where(place == 0, decay, jnp.where(place == 2, 0.0, 1.0))
         on_second = jnp.where(place == 1, decay, jnp.where(place == 3, 0.0, 1.0))
         mixing[:, h * wide:(h + 1) * wide] = jnp.where(first, on_first, on_second)
+        decays[:, lanes_of(h)] = decay_out_of(jnp.full((1, HD), rate[h], F32))
     for h in range(count):
-        decay_out = decay_out_of(rate[h])
         copies[1 + 2 * h].wait()
         copies[2 + 2 * h].wait()
-        key_dec = scaled(head(key_in, h), decay_out)
+        key_dec = scaled(head(key_in, h), head(decays, h))
         put_halves(keep, send, h, dot(key_dec, head(value_in, h), 0, 0), odd)
 
 
@@ -115,13 +125,29 @@
 def intra_kernel(rows, queries, keys, values, attn, intra):
     for h in range(queries.shape[1] // HD):
         scores = dot(head(queries, h), head(keys, h), 1, 1)
-        weights = (scores * mask_of(rows[h:h + 1, :])).astype(BF16)
+        weights = (scores * mask_of(rows[h:h + 1, :], decay_in_of(short(rows, h)))).astype(BF16)
         attn[h] = weights
         intra[:, lanes_of(h)] = dot(weights, head(values, h), 1, 0)
 
 
+def factors(mixing, backward):
+    return [mixing[i:i + 1, :] for i in range(4 * backward, 4 * backward + 4)]
+
+
+def join_kernel(backward, mixing, keep, got, total):
+    own, coming = factors(mixing, backward)[:2]
+    total[:, 0, :] = own * keep[...] + coming * got[...]
+
+
+def spread_kernel(backward, mixing, keep, got, prefix, mine, other):
+    own, coming, add_mine, add_other = factors(mixing, backward)
+    incoming = prefix[:, 0, :]
+    other[...] = own * incoming + add_other * keep[...]
+    mine[...] = coming * incoming + add_mine * got[...]
+
+
 def scan_kernel(backward, rows, totals, prefix):
-    chips, width = totals.shape
+    chips, one, width = totals.shape
     count = width * chips * 2 // HD // HD
     wide = width // count
     row = lax.broadcasted_iota(jnp.int32, (chips, chips), 0)
@@ -131,8 +157,8 @@
         lanes = slice(h * wide, (h + 1) * wide)
         rate = rows[h:h + 1, 0:chips]
         weight = jnp.where(far >= 0.0, jnp.exp(-(rate * (2.0 * BLOCK)) * jnp.maximum(far, 0.0)), 0.0)
-        prefix[:, lanes] = lax.dot_general(
-            weight, totals[:, lanes], (((1,), (0,)), ((), ())),
+        prefix[:, 0, lanes] = lax.dot_general(
+            weight, totals[:, 0, lanes], (((1,), (0,)), ((), ())),
             precision=lax.Precision.HIGHEST, preferred_element_type=F32)
 
 
@@ -171,40 +197,49 @@
         put_halves(keep, send, h, dot(query_dec, grad, 0, 0), odd)
 
 
-def local_kernel(rows, queries, keys, values, d_out, held, query_grad, key_part):
-    for h in range(queries.shape[1] // HD):
+def local_kernel(rows, keys, values, d_out, held, query_grad, back_attn):
+    for h in range(keys.shape[1] // HD):
         grad = head(d_out, h)
-        back = (dot(grad, head(values, h), 1, 1) * mask_of(rows[h:h + 1, :])).astype(BF16)
-        grad_dec = scaled(grad, decay_in_of(short(rows, h)))
+        decay_in = decay_in_of(short(rows, h))
+        back = (dot(grad, head(values, h), 1, 1) * mask_of(rows[h:h + 1, :], decay_in)).astype(BF16)
+        back_attn[h] = back
         query_grad[:, lanes_of(h)] = (
-            dot(back, head(keys, h), 1, 0) + dot(grad_dec, head(held, h), 1, 1)).astype(BF16)
-        key_part[:, lanes_of(h)] = dot(back, head(queries, h), 0, 0)
-
-
-def value_kernel(attn, d_out, value_part):
+            dot(back, head(keys, h), 1, 0) + dot(scaled(grad, decay_in), head(held, h), 1, 1)).astype(BF16)
+
+
+def parts_kernel(queries, attn, back_attn, d_out, key_part, value_part):
     for h in range(attn.shape[0]):
+        key_part[:, lanes_of(h)] = dot(back_attn[h], head(queries, h), 0, 0)
         value_part[:, lanes_of(h)] = dot(attn[h], head(d_out, h), 0, 0)
 
 
-def last_kernel(rows, mixing, keys, values, mine, other, key_part, value_part, key_grad, value_grad):
+def last_kernel(rows, mixing, keys, values, mine, other, key_part, value_part,
+                key_grad, value_grad, key_out, value_out, sems):
     odd = odd_of(mixing)
+    copies = []
     for h in range(keys.shape[1] // HD):
         later = get_state(mine, other, h, odd)
         decay_out = decay_out_of(short(rows, h))
         value_dec = scaled(head(values, h), decay_out)
         key_dec = scaled(head(keys, h), decay_out)
-        key_grad[:, lanes_of(h)] = (head(key_part, h) + dot(value_dec, later, 1, 1)).astype(BF16)
-        value_grad[:, lanes_of(h)] = (head(value_part, h) + dot(key_dec, later, 1, 0)).astype(BF16)
-
-
-def call(body, name, args, shapes, specs=None, scratch=(), flops=0):
+        key_out[:, lanes_of(h)] = (head(key_part, h) + dot(value_dec, later, 1, 1)).astype(BF16)
+        value_out[:, lanes_of(h)] = (head(value_part, h) + dot(key_dec, later, 1, 0)).astype(BF16)
+        for which, (source, target) in enumerate(((key_out, key_grad), (value_out, value_grad))):
+            copies.append(pltpu.make_async_copy(
+                source.at[:, lanes_of(h)], target.at[:, lanes_of(h)], sems.at[2 * h + which]))
+            copies[-1].start()
+    for copy in copies:
+        copy.wait()
+
+
+def call(body, name, args, shapes, specs=None, scratch=(), flops=0, into=VMEM):
     outs = [jax.ShapeDtypeStruct(shape, kind) for shape, kind in shapes]
     moved = sum(a.size * a.dtype.itemsize for a in args)
     return pl.pallas_call(
         body,
         out_shape=outs if len(outs) > 1 else outs[0],
         in_specs=specs or [VMEM] * len(args),
-        out_specs=[VMEM] * len(outs) if len(outs) > 1 else VMEM,
+        out_specs=[into] * len(outs) if len(outs) > 1 else into,
         scratch_shapes=list(scratch),
         compiler_params=pltpu.CompilerParams(vmem_limit_bytes=16 * 1024 * 1024),
         cost_estimate=pl.CostEstimate(flops=flops, bytes_accessed=moved, transcendentals=0),
@@ -216,20 +251,22 @@
     chips, width = keep.shape
     partners = [(i, i ^ 1) for i in range(2 * chips)]
     rings = [[2 * i + c for i in range(chips)] for c in range(2)]
-    own, coming, add_mine, add_other = (mixing[4 * backward + i][None] for i in range(4))
+    flat = ((chips, 1, width), F32)
 
     got = lax.ppermute(send, "ctx", partners)
-    beside_first = beside_first()
-    got, beside_first = lax.optimization_barrier((got, beside_first))
-    total = own * keep + coming * got
+    first = beside_first()
+    got, first = lax.optimization_barrier((got, first))
+    total = call(functools.partial(join_kernel, backward), "join", [mixing, keep, got], [flat])
     total = lax.all_to_all(total, "ctx", 0, 0, tiled=True, axis_index_groups=rings)
-    prefix = call(functools.partial(scan_kernel, backward), "scan", [rows, total], [((chips, width), F32)])
+    prefix = call(functools.partial(scan_kernel, backward), "scan", [rows, total], [flat])
     prefix = lax.all_to_all(prefix, "ctx", 0, 0, tiled=True, axis_index_groups=rings)
-    other = lax.ppermute(own * prefix + add_other * keep, "ctx", partners)
-    mine = coming * prefix + add_mine * got
-    beside_last = beside_last()
-    other, beside_last = lax.optimization_barrier((other, beside_last))
-    return mine, other, beside_first, beside_last
+    mine, other = call(
+        functools.partial(spread_kernel, backward), "spread", [mixing, keep, got, prefix],
+        [((chips, width), F32)] * 2)
+    other = lax.ppermute(other, "ctx", partners)
+    last = beside_last(first)
+    other, last = lax.optimization_barrier((other, last))
+    return mine, other, first, last
 
 
 def per_device(queries, keys, values, out_grad, rates, gain):
@@ -246,26 +283,31 @@
         [half, half, ((8, BLOCK), F32), ((8, half[0][1]), F32)],
         specs=[HBM] * 3,
         scratch=[pltpu.SMEM((count,), F32), pltpu.VMEM((BLOCK, width), BF16), pltpu.VMEM((BLOCK, width), BF16),
+                 pltpu.VMEM((BLOCK, width), F32),
                  pltpu.SemaphoreType.DMA((2 * count + 1,))])
-    mine, other, (attn, intra), unused = scan(
-        keep, send, rows, mixing,
-        lambda: call(intra_kernel, "intra", [rows, queries, keys, values],
-                     [((count, BLOCK, BLOCK), BF16), wide32], flops=4 * BLOCK * BLOCK * width),
-        lambda: (), False)
+    mine, other, unused, (attn, intra) = scan(
+        keep, send, rows, mixing, lambda: (),
+        lambda first: call(intra_kernel, "intra", [rows, queries, keys, values],
+                           [((count, BLOCK, BLOCK), BF16), wide32], flops=4 * BLOCK * BLOCK * width),
+        False)
     out, held, sums = call(
         out_kernel, "out", [rows, mixing, queries, out_grad, gain, intra, mine, other],
         [wide32, ((HD, width), BF16), ((ranks, 2, BLOCK), F32)])
     sums = lax.all_to_all(sums, "head", 0, 0, tiled=True)
     d_out, keep, send = call(
         grad_kernel, "grad", [rows, mixing, queries, out_grad, gain, out, sums], [wide16, half, half])
-    mine, other, (query_grad, key_part), value_part = scan(
+    mine, other, (query_grad, unused), (key_part, value_part) = scan(
         keep, send, rows, mixing,
-        lambda: call(local_kernel, "local", [rows, queries, keys, values, d_out, held], [wide16, wide32],
-                     flops=6 * BLOCK * BLOCK * width),
-        lambda: call(value_kernel, "value", [attn, d_out], [wide32], flops=2 * BLOCK * BLOCK * width),
+        lambda: call(local_kernel, "local", [rows, keys, values, d_out, held],
+                     [wide16, ((count, BLOCK, BLOCK), BF16)], flops=4 * BLOCK * BLOCK * width),
+        lambda first: call(parts_kernel, "parts", [queries, attn, first[1], d_out], [wide32, wide32],
+                           flops=4 * BLOCK * BLOCK * width),
         True)
     key_grad, value_grad = call(
-        last_kernel, "last", [rows, mixing, keys, values, mine, other, key_part, value_part], [wide16, wide16])
+        last_kernel, "last", [rows, mixing, keys, values, mine, other, key_part, value_part], [wide16, wide16],
+        scratch=[pltpu.VMEM((BLOCK, width), BF16), pltpu.VMEM((BLOCK, width), BF16),
+                 pltpu.SemaphoreType.DMA((2 * count,))],
+        into=HBM)
     return query_grad, key_grad, value_grad
 
 

time: 105 us -> 103 us (0.981)
  local copies, waits for them, and re-layouts: 1.8 us -> 0.05 us
    pallas_call x9 -> x13, Pallas kernels: 7.93 us -> 7.76 us  [call(): pl.pallas_call(body, out_shape=outs if len(outs) > 1 else outs[0], in_spe...]
  transfers between devices with their start and end apart: 4 -> 4, of which waited for: 2 -> 3; matrix products, arithmetic and copies ran while one was open for 0% -> 0% of each run, Pallas kernels for 3% -> 3%
where the time goes in v3:
time: 103 us
  blocking collectives  70.8 us (69%)
  starting transfers between devices  21.8 us (21%)
  Pallas kernels  7.76 us (8%)
  waiting for transfers between devices  1.65 us (2%)
    all_to_all x2, blocking collectives, scan(): lax.all_to_all(total, 'ctx', 0, 0, tiled=True, axis_index_groups=rings)  30.6 us
    all_to_all x2, blocking collectives, scan(): lax.all_to_all(prefix, 'ctx', 0, 0, tiled=True, axis_index_groups=rings)  27 us
    all_to_all x1, blocking collectives, per_device(): sums = lax.all_to_all(sums, 'head', 0, 0, tiled=True)  13.2 us
    ppermute x2, starting transfers between devices, scan(): got = lax.ppermute(send, 'ctx', partners)  12.5 us
    ppermute x2, starting transfers between devices, scan(): other = lax.ppermute(other, 'ctx', partners)  9.36 us
    pallas_call x13, Pallas kernels, call(): pl.pallas_call(body, out_shape=outs if len(outs) > 1 else outs[0], in_spe...  7.76 us
  transfers between devices with their start and end apart: 4, of which 3 were waited for; matrix products, arithmetic and copies ran while one was open for 0% of the time, Pallas kernels for 3%

profile of v3, /device:TPU:1, one launch (start us, length us, event | category | flops | bytes accessed | tf_op | source)
XLA Modules:
  0.0 102.9 jit_solution(4387918976060066825)
XLA Ops:
  0.6 2.0 %kv.1 = (f32[32,1280]{1,0:T(8,128)S(1)}, f32[32,1280]{1,0:T(8,128)S(1)}, f32[8,256]{1,0:T(8,128)S(1)}, f32[8,1280]{1,0:T(8,128)S(1)}) custom-call(f32[5]{0:T(128)} %rates.1, bf16[256,640]{1,0:T(8,128)(2,1)} %keys.7, bf16[256,640]{1,0:T(8,128)(2,1)} %values.7), custom_call_target="tpu_custom_call" | custom-call | bytes 655380 | tf_op jit(solution)/shard_map/kv/pallas_call | solution.py:238
  2.7 8.8 %collective-permute-start = (f32[32,1280]{1,0:T(8,128)S(1)}, f32[32,1280]{1,0:T(8,128)S(1)}, u32[]{:S(2)}, u32[]{:S(2)}) collective-permute-start(f32[32,1280]{1,0:T(8,128)S(1)} %get-tuple-element.37), channel_id=1, source_target_pairs={{0,8},{8,0},{16,24},{24,16},{32,40},{40,32},{48,56},{56,48},{64,72... | collective-permute-start | bytes 491528 | tf_op jit(solution)/shard_map/ppermute | solution.py:256
  11.4 1.0 collective-permute-done.got
  12.5 0.1 join.2
  12.5 17.4 %all_to_all.25.totals = f32[32,1,1280]{2,1,0:T(1,128)S(1)} all-to-all(f32[32,1,1280]{2,1,0:T(1,128)S(1)} %join.2), channel_id=1, replica_groups={{0,16,32,48,64,80,96,112,128,144,160,176,192,208,224,240,256,272,288,30..., dimensions={0} | all-to-all | bytes 327680 | tf_op jit(solution)/shard_map/all_to_all | solution.py:260
  29.9 0.0 copy-start.2
  29.9 0.3 scan.2
  30.2 0.0 copy-start.1
  30.2 13.6 %all_to_all.26.prefix = f32[32,1,1280]{2,1,0:T(1,128)S(1)} all-to-all(f32[32,1,1280]{2,1,0:T(1,128)S(1)} %scan.2), channel_id=1, replica_groups={{0,16,32,48,64,80,96,112,128,144,160,176,192,208,224,240,256,272,288,30..., dimensions={0} | all-to-all | bytes 327680 | tf_op jit(solution)/shard_map/all_to_all | solution.py:262
  43.8 0.0 copy-start.4
  43.8 0.0 copy-start
  43.8 0.1 spread.2
  43.9 4.8 %collective-permute-start.1 = (f32[32,1280]{1,0:T(8,128)S(1)}, f32[32,1280]{1,0:T(8,128)S(1)}, u32[]{:S(2)}, u32[]{:S(2)}) collective-permute-start(f32[32,1280]{1,0:T(8,128)S(1)} %get-tuple-element.38), channel_id=1, source_target_pairs={{0,8},{8,0},{16,24},{24,16},{32,40},{40,32},{48,56},{56,48},{64,72... | collective-permute-start | bytes 491528 | tf_op jit(solution)/shard_map/ppermute | solution.py:266
  48.7 0.0 copy-done.4
  48.7 0.0 copy-done.2
  48.7 0.0 copy-done.1
  48.8 0.0 copy-done
  48.8 0.0 copy-start.3
  48.8 0.7 intra.1
  49.5 0.2 collective-permute-done.1.other
  49.7 0.0 copy-done.3
  49.7 0.5 out.1
  50.2 13.2 %all_to_all.27.sums = f32[8,2,256]{2,1,0:T(2,128)S(1)} all-to-all(f32[8,2,256]{2,1,0:T(2,128)S(1)} %get-tuple-element.45), channel_id=1, replica_groups=mesh['ctx'=64,'head'=8] {'head'}, dimensions={0} | all-to-all | bytes 32768 | tf_op jit(solution)/shard_map/all_to_all | solution.py:296
  63.4 0.5 grad.1
  63.9 3.7 %collective-permute-start.2 = (f32[32,1280]{1,0:T(8,128)S(1)}, f32[32,1280]{1,0:T(8,128)S(1)}, u32[]{:S(2)}, u32[]{:S(2)}) collective-permute-start(f32[32,1280]{1,0:T(8,128)S(1)} %get-tuple-element.46), channel_id=1, source_target_pairs={{0,8},{8,0},{16,24},{24,16},{32,40},{40,32},{48,56},{56,48},{64,72... | collective-permute-start | bytes 491528 | tf_op jit(solution)/shard_map/ppermute | solution.py:256
  67.6 1.5 %local.1 = (bf16[256,640]{1,0:T(8,128)(2,1)}, bf16[5,256,256]{2,1,0:T(8,128)(2,1)S(1)}) custom-call(f32[8,256]{1,0:T(8,128)S(1)} %get-tuple-element.34.rows, bf16[256,640]{1,0:T(8,128)(2,1)S(1)} %copy-done, bf16[256,640]{1,0:T(8,128)(2,1)S(1)} %copy-done.1, bf16[256,640]{1,0:T(8,128)(2,1)S(1)} %get-tuple-element.47.d_out, ...), custom_call_target="tpu_custom_call" | custom-call | flops 167772160 | bytes 1155072 | tf_op jit(solution)/shard_map/local/pallas_call | solution.py:238
  69.2 0.0 collective-permute-done.2.got
  69.2 0.1 join.3
  69.2 13.2 %all_to_all.28.totals = f32[32,1,1280]{2,1,0:T(1,128)S(1)} all-to-all(f32[32,1,1280]{2,1,0:T(1,128)S(1)} %join.3), channel_id=1, replica_groups={{0,16,32,48,64,80,96,112,128,144,160,176,192,208,224,240,256,272,288,30..., dimensions={0} | all-to-all | bytes 327680 | tf_op jit(solution)/shard_map/all_to_all | solution.py:260
  82.4 0.3 scan.3
  82.7 13.4 %all_to_all.29.prefix = f32[32,1,1280]{2,1,0:T(1,128)S(1)} all-to-all(f32[32,1,1280]{2,1,0:T(1,128)S(1)} %scan.3), channel_id=1, replica_groups={{0,16,32,48,64,80,96,112,128,144,160,176,192,208,224,240,256,272,288,30..., dimensions={0} | all-to-all | bytes 327680 | tf_op jit(solution)/shard_map/all_to_all | solution.py:262
  96.1 0.1 spread.3
  96.2 4.5 %collective-permute-start.3 = (f32[32,1280]{1,0:T(8,128)S(1)}, f32[32,1280]{1,0:T(8,128)S(1)}, u32[]{:S(2)}, u32[]{:S(2)}) collective-permute-start(f32[32,1280]{1,0:T(8,128)S(1)} %get-tuple-element.55), channel_id=1, source_target_pairs={{0,8},{8,0},{16,24},{24,16},{32,40},{40,32},{48,56},{56,48},{64,72... | collective-permute-start | bytes 491528 | tf_op jit(solution)/shard_map/ppermute | solution.py:266
  100.8 0.6 parts.1
  101.3 0.4 collective-permute-done.3.other
  101.8 1.1 %last.1 = (bf16[256,640]{1,0:T(8,128)(2,1)}, bf16[256,640]{1,0:T(8,128)(2,1)}) custom-call(f32[8,256]{1,0:T(8,128)S(1)} %get-tuple-element.34.rows, f32[8,1280]{1,0:T(8,128)S(1)} %get-tuple-element.35.mixing, bf16[256,640]{1,0:T(8,128)(2,1)S(1)} %copy-done, bf16[256,640]{1,0:T(8,128)(2,1)S(1)} %copy-done.1, f32[32,1280]{1,0:T(8,128)S(1)} %get-tuple-element.54.mine, ...), custom_call_target="tpu_custom_call" | custom-call | bytes 2342912 | tf_op jit(solution)/shard_map/last/pallas_call | solution.py:238
  (1 shorter events, 0.0 us)
Async XLA Ops:
  2.7 9.8 %collective-permute-start = (f32[32,1280]{1,0:T(8,128)S(1)}, f32[32,1280]{1,0:T(8,128)S(1)}, u32[]{:S(2)}, u32[]{:S(2)}) collective-permute-start(f32[32,1280]{1,0:T(8,128)S(1)} %get-tuple-element.37), channel_id=1, source_target_pairs={{0,8},{8,0},{16,24},{24,16},{32,40},{40,32},{48,56},{56,48},{64,72... | collective-permute-start | bytes 491528 | tf_op jit(solution)/shard_map/ppermute | solution.py:256
  29.9 18.8 %copy-start.2 = (bf16[256,640]{1,0:T(8,128)(2,1)S(1)}, bf16[256,640]{1,0:T(8,128)(2,1)}, u32[]{:S(2)}) copy-start(bf16[256,640]{1,0:T(8,128)(2,1)} %queries.7) | copy-start | bytes 983044
  30.2 18.5 %copy-start.1 = (bf16[256,640]{1,0:T(8,128)(2,1)S(1)}, bf16[256,640]{1,0:T(8,128)(2,1)}, u32[]{:S(2)}) copy-start(bf16[256,640]{1,0:T(8,128)(2,1)} %values.7) | copy-start | bytes 983044
  43.8 4.9 %copy-start.4 = (f32[640]{0:T(1024)S(1)}, f32[640]{0:T(1024)}, u32[]{:S(2)}) copy-start(f32[640]{0:T(1024)} %param.11) | copy-start | bytes 7684
  43.8 5.0 %copy-start = (bf16[256,640]{1,0:T(8,128)(2,1)S(1)}, bf16[256,640]{1,0:T(8,128)(2,1)}, u32[]{:S(2)}) copy-start(bf16[256,640]{1,0:T(8,128)(2,1)} %keys.7) | copy-start | bytes 983044
  43.9 5.8 %collective-permute-start.1 = (f32[32,1280]{1,0:T(8,128)S(1)}, f32[32,1280]{1,0:T(8,128)S(1)}, u32[]{:S(2)}, u32[]{:S(2)}) collective-permute-start(f32[32,1280]{1,0:T(8,128)S(1)} %get-tuple-element.38), channel_id=1, source_target_pairs={{0,8},{8,0},{16,24},{24,16},{32,40},{40,32},{48,56},{56,48},{64,72... | collective-permute-start | bytes 491528 | tf_op jit(solution)/shard_map/ppermute | solution.py:266
  48.8 1.0 copy-start.3
  63.9 5.2 %collective-permute-start.2 = (f32[32,1280]{1,0:T(8,128)S(1)}, f32[32,1280]{1,0:T(8,128)S(1)}, u32[]{:S(2)}, u32[]{:S(2)}) collective-permute-start(f32[32,1280]{1,0:T(8,128)S(1)} %get-tuple-element.46), channel_id=1, source_target_pairs={{0,8},{8,0},{16,24},{24,16},{32,40},{40,32},{48,56},{56,48},{64,72... | collective-permute-start | bytes 491528 | tf_op jit(solution)/shard_map/ppermute | solution.py:256
  96.2 5.5 %collective-permute-start.3 = (f32[32,1280]{1,0:T(8,128)S(1)}, f32[32,1280]{1,0:T(8,128)S(1)}, u32[]{:S(2)}, u32[]{:S(2)}) collective-permute-start(f32[32,1280]{1,0:T(8,128)S(1)} %get-tuple-element.55), channel_id=1, source_target_pairs={{0,8},{8,0},{16,24},{24,16},{32,40},{40,32},{48,56},{56,48},{64,72... | collective-permute-start | bytes 491528 | tf_op jit(solution)/shard_map/ppermute | solution.py:266

commit v4 on v3

v4 whole, which is shorter than its diff:
```python
import functools

import jax
import jax.numpy as jnp
from jax import lax
from jax.experimental import pallas as pl
from jax.experimental.pallas import tpu as pltpu
from jax.sharding import PartitionSpec as P

HD = 128
HEADS = 40
BLOCK = 256
epsilon = 1e-05

HALF = HD // 2
F32 = jnp.float32
BF16 = jnp.bfloat16
VMEM = pl.BlockSpec(memory_space=pltpu.VMEM)
HBM = pl.BlockSpec(memory_space=pltpu.HBM)


def dot(a, b, ca, cb):
    return lax.dot_general(a, b, (((ca,), (cb,)), ((), ())), preferred_element_type=F32)


def lanes_of(h):
    return slice(h * HD, (h + 1) * HD)


def head(ref, h):
    return ref[:, lanes_of(h)]


def decay_in_of(rate):
    place = lax.broadcasted_iota(jnp.int32, (8, HD), 0).astype(F32)
    table = jnp.exp(-rate * (place + 1.0))
    while table.shape[0] < BLOCK:
        step = jnp.exp(jnp.full((1, HD), -float(table.shape[0]), F32) * rate)
        table = jnp.concatenate([table, table * step], axis=0)
    return table


def decay_out_of(rate):
    place = lax.broadcasted_iota(jnp.int32, (8, HD), 0).astype(F32)
    table = jnp.exp(-rate * (7.0 - place))
    while table.shape[0] < BLOCK:
        step = jnp.exp(jnp.full((1, HD), -float(table.shape[0]), F32) * rate)
        table = jnp.concatenate([table * step, table], axis=0)
    return table


def mask_of(rates, decay_in):
    row = lax.broadcasted_iota(jnp.int32, (BLOCK, BLOCK), 0)
    col = lax.broadcasted_iota(jnp.int32, (BLOCK, BLOCK), 1)
    place = lax.broadcasted_iota(jnp.int32, (1, BLOCK), 1).astype(F32)
    growth = jnp.exp(rates * (place + 1.0))
    both = jnp.concatenate([decay_in, decay_in], axis=1) * growth
    return jnp.where(row >= col, both, 0.0)


def short(rows, h):
    return rows[h:h + 1, 0:HD]


def scaled(array, scale):
    return (array.astype(F32) * scale).astype(BF16)


def put_halves(keep, send, h, state, odd):
    chips = keep.shape[0]
    share = HD // 2 // chips
    low, high = state[:HD // 2], state[HD // 2:]
    mine, other = jnp.where(odd, high, low), jnp.where(odd, low, high)
    for r in range(share):
        lane = (h * share + r) * HD
        keep[:, lane:lane + HD] = mine[r * chips:(r + 1) * chips]
        send[:, lane:lane + HD] = other[r * chips:(r + 1) * chips]


def put_half(ref, h, state):
    chips = ref.shape[0]
    share = HD // 2 // chips
    for r in range(share):
        lane = (h * share + r) * HD
        ref[:, lane:lane + HD] = state[r * chips:(r + 1) * chips]


def get_half(ref, h):
    chips = ref.shape[0]
    share = HD // 2 // chips
    return jnp.concatenate([ref[:, lanes_of(h * share + r)] for r in range(share)], axis=0)


def rows_of(h, size, start=0):
    return slice(start + h * size, start + (h + 1) * size)


def whole(mine, other, odd):
    low, high = jnp.where(odd, other, mine), jnp.where(odd, mine, other)
    return jnp.concatenate([low, high], axis=0)


def get_state(mine, other, h, odd):
    return whole(get_half(mine, h), get_half(other, h), odd).astype(BF16)


def kv_kernel(rates, keys, values, queries, out_grad, keep, send, rows, mixing, key_in, value_in, query_in, grad_in,
              rate, decays, sems):
    count = rates.shape[0]
    odd = lax.rem(lax.axis_index("ctx"), 2) == 1
    copies = [pltpu.make_async_copy(rates, rate, sems.at[0])]
    for h in range(count):
        for source, target in ((keys, key_in), (values, value_in)):
            copies.append(pltpu.make_async_copy(
                source.at[:, lanes_of(h)], target.at[:, lanes_of(h)], sems.at[len(copies)]))
    for source, target in ((queries, query_in), (out_grad, grad_in)):
        copies.append(pltpu.make_async_copy(source, target, sems.at[len(copies)]))
    for copy in copies:
        copy.start()
    copies[0].wait()
    wide = mixing.shape[1] // count
    index = lax.broadcasted_iota(jnp.int32, (8, wide), 0)
    for h in range(count):
        rows[h:h + 1, :] = jnp.full((1, BLOCK), rate[h], F32)
        decay = jnp.exp(jnp.full((8, wide), -rate[h] * BLOCK, F32))
        place = lax.rem(index, 4)
        later = index >= 4
        first = later == odd
        on_first = jnp.where(place == 0, decay, jnp.where(place == 2, 0.0, 1.0))
        on_second = jnp.where(place == 1, decay, jnp.where(place == 3, 0.0, 1.0))
        mixing[:, h * wide:(h + 1) * wide] = jnp.where(first, on_first, on_second)
        decays[:, lanes_of(h)] = decay_out_of(jnp.full((1, HD), rate[h], F32))
    for h in range(count):
        copies[1 + 2 * h].wait()
        copies[2 + 2 * h].wait()
        key_dec = scaled(head(key_in, h), head(decays, h))
        put_halves(keep, send, h, dot(head(value_in, h), key_dec, 0, 0), odd)
    for copy in copies[1 + 2 * count:]:
        copy.wait()


def odd_of(mixing, width=HD):
    return mixing[2:3, 0:width] > 0.5


def intra_kernel(rows, mixing, queries, keys, values, out_grad, gain, attn, query_t, intra_t, weighted_t, partner):
    odd = odd_of(mixing, BLOCK)
    count = queries.shape[1] // HD
    for h in range(count):
        decay_in = decay_in_of(short(rows, h))
        scores = dot(head(queries, h), head(keys, h), 1, 1)
        weights = (scores * mask_of(rows[h:h + 1, :], decay_in)).astype(BF16)
        attn[h] = weights
        query_dec = scaled(head(queries, h), decay_in).astype(F32).T
        query_t[rows_of(h, HD), :] = query_dec.astype(BF16)
        partner[rows_of(h, HD), :] = query_dec
        intra = dot(head(values, h), weights, 0, 1)
        weighted = (head(out_grad, h).astype(F32) * head(gain, h)).T
        start = count * HD
        for array, target in ((intra, intra_t), (weighted, weighted_t)):
            low, high = array[:HALF], array[HALF:]
            target[rows_of(h, HALF), :] = jnp.where(odd, high, low)
            partner[rows_of(h, HALF, start), :] = jnp.where(odd, low, high)
            start += count * HALF


def factors(mixing, backward):
    return [mixing[i:i + 1, :] for i in range(4 * backward, 4 * backward + 4)]


def join_kernel(backward, mixing, keep, got, total):
    own, coming = factors(mixing, backward)[:2]
    total[:, 0, :] = own * keep[...] + coming * got[...]


def spread_kernel(backward, mixing, base, prefix, mine, other):
    own, coming, add_mine, add_other = factors(mixing, backward)
    incoming = prefix[:, 0, :]
    other[...] = own * incoming + add_other * base[...]
    mine[...] = coming * incoming + add_mine * base[...]


def scan_kernel(backward, rows, totals, prefix):
    chips, one, width = totals.shape
    count = width * chips * 2 // HD // HD
    wide = width // count
    row = lax.broadcasted_iota(jnp.int32, (chips, chips), 0)
    col = lax.broadcasted_iota(jnp.int32, (chips, chips), 1)
    far = ((col - row - 1) if backward else (row - col - 1)).astype(F32)
    for h in range(count):
        lanes = slice(h * wide, (h + 1) * wide)
        rate = rows[h:h + 1, 0:chips]
        weight = jnp.where(far >= 0.0, jnp.exp(-(rate * (2.0 * BLOCK)) * jnp.maximum(far, 0.0)), 0.0)
        prefix[:, 0, lanes] = lax.dot_general(
            weight, totals[:, 0, lanes], (((1,), (0,)), ((), ())),
            precision=lax.Precision.HIGHEST, preferred_element_type=F32)


def fold(array):
    return jnp.sum(array.reshape(HALF // 8, 8, BLOCK), axis=0)


def blocks_of(h, count, query_t, intra_t, weighted_t, partner):
    mine = (query_t[rows_of(h, HD), :], intra_t[rows_of(h, HALF), :], weighted_t[rows_of(h, HALF), :])
    other = (partner[rows_of(h, HD), :].astype(BF16), partner[rows_of(h, HALF, count * HD), :],
             partner[rows_of(h, HALF, count * (HD + HALF)), :])
    return mine, other


def out_kernel(mixing, keep, got, prefix, query_t, intra_t, weighted_t, partner, out, held, sums):
    chips, width = keep.shape
    count = query_t.shape[0] // HD
    wide = width // count
    share = wide // HD
    sums_of = [[jnp.zeros((8, BLOCK), F32) for _ in range(2)] for _ in range(2)]
    for h in range(count):
        own, coming, add_mine, add_other = (row[:, h * wide:h * wide + HD] for row in factors(mixing, False))
        incoming = jnp.concatenate([prefix[:, 0, lanes_of(h * share + r)] for r in range(share)], axis=0)
        states = (coming * incoming + add_mine * get_half(got, h), own * incoming + add_other * get_half(keep, h))
        for which, (query, intra, weighted) in enumerate(blocks_of(h, count, query_t, intra_t, weighted_t, partner)):
            state = states[which].astype(BF16)
            held[which, rows_of(h, HALF), :] = state.astype(F32)
            result = intra + dot(state, query, 1, 0)
            out[which, rows_of(h, HALF), :] = result
            sums_of[which][0] = sums_of[which][0] + fold(result * result)
            sums_of[which][1] = sums_of[which][1] + fold(weighted * result)
    odd = odd_of(mixing, BLOCK)
    mine, other = ([jnp.sum(part, axis=0, keepdims=True) for part in parts] for parts in sums_of)
    even_block = [jnp.where(odd, b, a) for a, b in zip(mine, other)]
    odd_block = [jnp.where(odd, a, b) for a, b in zip(mine, other)]
    both = jnp.concatenate(even_block + odd_block, axis=0)
    for peer in range(sums.shape[0]):
        sums[peer] = both


def pack_kernel(grad_t, held, exchange):
    exchange[:, 0:BLOCK] = grad_t[1].astype(F32)
    exchange[:, BLOCK:BLOCK + HD] = held[1]


def grad_kernel(mixing, sums, out, query_t, intra_t, weighted_t, partner, total, base, grad_t):
    odd = odd_of(mixing, BLOCK)
    count = query_t.shape[0] // HD
    first = mixing[7:8, 0:HD] > 0.5
    chips, one, width = total.shape
    wide = width // count
    share = wide // HD
    summed = jnp.sum(sums[...], axis=0)
    even_block, odd_block = summed[0:2], summed[2:4]
    scales = []
    for block in (jnp.where(odd, odd_block, even_block), jnp.where(odd, even_block, odd_block)):
        inverse = lax.rsqrt(block[0:1] / (HEADS * HD) + epsilon)
        scales.append((inverse, inverse * inverse * inverse * block[1:2] / (HEADS * HD)))
    for h in range(count):
        own, coming = (row[:, h * wide:h * wide + HD] for row in factors(mixing, True)[:2])
        terms = []
        for which, (query, intra, weighted) in enumerate(blocks_of(h, count, query_t, intra_t, weighted_t, partner)):
            inverse, factor = scales[which]
            grad = (weighted * inverse - out[which, rows_of(h, HALF), :] * factor).astype(BF16)
            grad_t[which, rows_of(h, HALF), :] = grad
            terms.append(dot(grad, query, 1, 1))
        put_half(base, h, jnp.where(first, terms[0], terms[1]))
        joined = own * terms[0] + coming * terms[1]
        for r in range(share):
            total[:, 0, lanes_of(h * share + r)] = joined[r * chips:(r + 1) * chips]


def local_kernel(rows, mixing, keys, values, grad_t, held, exchange, query_grad, back_attn, whole_grad):
    for h in range(keys.shape[1] // HD):
        place = lax.broadcasted_iota(jnp.int32, (1, BLOCK), 1).astype(F32)
        grad = whole(grad_t[0, rows_of(h, HALF), :].astype(F32), exchange[rows_of(h, HALF), 0:BLOCK], odd_of(mixing, BLOCK))
        state = whole(held[0, rows_of(h, HALF), :], exchange[rows_of(h, HALF), BLOCK:BLOCK + HD], odd_of(mixing))
        grad_dec = (grad * jnp.exp(-rows[h:h + 1, :] * (place + 1.0))).astype(BF16)
        grad = grad.astype(BF16)
        whole_grad[rows_of(h, HD), :] = grad
        mask = mask_of(rows[h:h + 1, :], decay_in_of(short(rows, h)))
        back = (dot(grad, head(values, h), 0, 1) * mask).astype(BF16)
        back_attn[h] = back
        query_grad[:, lanes_of(h)] = (
            dot(back, head(keys, h), 1, 0) + dot(grad_dec, state.astype(BF16), 0, 0)).astype(BF16)


def parts_kernel(queries, attn, back_attn, whole_grad, key_part, value_part):
    for h in range(attn.shape[0]):
        key_part[:, lanes_of(h)] = dot(back_attn[h], head(queries, h), 0, 0)
        value_part[:, lanes_of(h)] = dot(attn[h], whole_grad[rows_of(h, HD), :], 0, 1)


def last_kernel(rows, mixing, keys, values, mine, other, key_part, value_part,
                key_grad, value_grad, key_out, value_out, sems):
    odd = odd_of(mixing)
    copies = []
    for h in range(keys.shape[1] // HD):
        later = get_state(mine, other, h, odd)
        decay_out = decay_out_of(short(rows, h))
        value_dec = scaled(head(values, h), decay_out)
        key_dec = scaled(head(keys, h), decay_out)
        key_out[:, lanes_of(h)] = (head(key_part, h) + dot(value_dec, later, 1, 0)).astype(BF16)
        value_out[:, lanes_of(h)] = (head(value_part, h) + dot(key_dec, later, 1, 1)).astype(BF16)
        for which, (source, target) in enumerate(((key_out, key_grad), (value_out, value_grad))):
            copies.append(pltpu.make_async_copy(
                source.at[:, lanes_of(h)], target.at[:, lanes_of(h)], sems.at[2 * h + which]))
            copies[-1].start()
    for copy in copies:
        copy.wait()


def call(body, name, args, shapes, specs=None, scratch=(), flops=0, into=VMEM):
    outs = [jax.ShapeDtypeStruct(shape, kind) for shape, kind in shapes]
    moved = sum(a.size * a.dtype.itemsize for a in args)
    return pl.pallas_call(
        body,
        out_shape=outs if len(outs) > 1 else outs[0],
        in_specs=specs or [VMEM] * len(args),
        out_specs=[into] * len(outs) if len(outs) > 1 else into,
        scratch_shapes=list(scratch),
        compiler_params=pltpu.CompilerParams(vmem_limit_bytes=16 * 1024 * 1024),
        cost_estimate=pl.CostEstimate(flops=flops, bytes_accessed=moved, transcendentals=0),
        name=name,
    )(*args)


def per_device(queries, keys, values, out_grad, rates, gain):
    tokens, width = queries.shape
    count = rates.shape[0]
    chips = lax.axis_size("ctx") // 2
    ranks = lax.axis_size("head")
    lanes = count * HD * HALF // chips
    half, flat, rows_half = ((chips, lanes), F32), ((chips, 1, lanes), F32), ((count * HALF, BLOCK), F32)
    gain = gain.reshape(1, width)
    wide16, wide32 = ((BLOCK, width), BF16), ((BLOCK, width), F32)
    square = ((count, BLOCK, BLOCK), BF16)
    unit = BLOCK * BLOCK * width
    partners = [(i, i ^ 1) for i in range(2 * chips)]
    rings = [[2 * i + c for i in range(chips)] for c in range(2)]
    towers = [[(2 * i + c) * ranks + y for c in range(2) for y in range(ranks)] for i in range(chips)]

    def swap(array):
        return lax.ppermute(array, "ctx", partners)

    def spread_out(array):
        return lax.all_to_all(array, "ctx", 0, 0, tiled=True, axis_index_groups=rings)

    keep, send, rows, mixing, key_in, value_in, query_in, grad_in = call(
        kv_kernel, "kv", [pltpu.with_memory_space_constraint(a, pltpu.HBM) for a in (rates, keys, values, queries, out_grad)],
        [half, half, ((8, BLOCK), F32), ((8, lanes), F32)] + [wide16] * 4,
        specs=[HBM] * 5,
        scratch=[pltpu.SMEM((count,), F32), pltpu.VMEM((BLOCK, width), F32),
                 pltpu.SemaphoreType.DMA((2 * count + 3,))])
    got = swap(send)
    attn, query_t, intra_t, weighted_t, partner = call(
        intra_kernel, "intra", [rows, mixing, query_in, key_in, value_in, grad_in, gain],
        [square, ((width, BLOCK), BF16), rows_half, rows_half, ((2 * width, BLOCK), F32)], flops=4 * unit)
    got, partner = lax.optimization_barrier((got, partner))
    total = call(functools.partial(join_kernel, False), "join", [mixing, keep, got], [flat])
    total = spread_out(total)
    prefix = call(functools.partial(scan_kernel, False), "scan", [rows, total], [flat])
    prefix, partner = lax.optimization_barrier((prefix, partner))
    partner = swap(partner)
    prefix = spread_out(prefix)
    shared = [query_t, intra_t, weighted_t, partner]
    out, held, sums = call(
        out_kernel, "out", [mixing, keep, got, prefix] + shared,
        [((2, count * HALF, BLOCK), F32), ((2, count * HALF, HD), F32), ((2 * ranks, 4, BLOCK), F32)])
    sums = lax.all_to_all(sums, ("ctx", "head"), 0, 0, tiled=True, axis_index_groups=towers)
    total, base, grad_t = call(
        grad_kernel, "grad", [mixing, sums, out] + shared,
        [flat, half, ((2, count * HALF, BLOCK), BF16)])
    total = spread_out(total)
    exchange = swap(call(pack_kernel, "pack", [grad_t, held], [((count * HALF, BLOCK + HD), F32)], flops=4 * unit))
    prefix = spread_out(call(functools.partial(scan_kernel, True), "scan", [rows, total], [flat]))
    mine, other = call(
        functools.partial(spread_kernel, True), "spread", [mixing, base, prefix], [half, half])
    tied, other = lax.optimization_barrier((rows, other))
    other = swap(other)
    query_grad, back_attn, whole_grad = call(
        local_kernel, "local", [tied, mixing, keys, values, grad_t, held, exchange],
        [wide16, square, ((width, BLOCK), BF16)], flops=4 * unit)
    key_part, value_part = call(
        parts_kernel, "parts", [queries, attn, back_attn, whole_grad], [wide32, wide32], flops=4 * unit)
    other, key_part, value_part = lax.optimization_barrier((other, key_part, value_part))
    key_grad, value_grad = call(
        last_kernel, "last", [rows, mixing, keys, values, mine, other, key_part, value_part], [wide16, wide16],
        scratch=[pltpu.VMEM((BLOCK, width), BF16), pltpu.VMEM((BLOCK, width), BF16),
                 pltpu.SemaphoreType.DMA((2 * count,))],
        into=HBM)
    return query_grad, key_grad, value_grad


def solution(mesh):
    spec = P("ctx", "head")
    return jax.shard_map(
        per_device, mesh=mesh, in_specs=(spec, spec, spec, spec, P("head"), P("head")),
        out_specs=(spec, spec, spec), check_vma=False)
```

time: 103 us -> 101 us (0.981)
  blocking collectives: 70.8 us -> 60.2 us
  waiting for transfers between devices: 1.65 us -> 7.11 us
  starting transfers between devices: 21.8 us -> 24.5 us
    all_to_all x5 -> x4, blocking collectives: 70.8 us -> 60.2 us  [the longest x3 44.3 us: spread_out(): lax.all_to_all(array, 'ctx', 0, 0, tiled=True, axis_index_groups=rings)]
    all_to_all x0 -> x1, waiting for transfers between devices: none -> 6.79 us  [spread_out(): lax.all_to_all(array, 'ctx', 0, 0, tiled=True, axis_index_groups=rings)]
    all_to_all x0 -> x1, starting transfers between devices: none -> 4 us  [spread_out(): lax.all_to_all(array, 'ctx', 0, 0, tiled=True, axis_index_groups=rings)]
    ppermute x4, starting transfers between devices: 21.8 us -> 20.5 us  [swap(): return lax.ppermute(array, 'ctx', partners)]
    ppermute x4, waiting for transfers between devices: 1.65 us -> 0.32 us  [swap(): return lax.ppermute(array, 'ctx', partners)]
    pallas_call x13 -> x12, Pallas kernels: 7.76 us -> 8.05 us  [call(): pl.pallas_call(body, out_shape=outs if len(outs) > 1 else outs[0], in_spe...]
  transfers between devices with their start and end apart: 4 -> 5, of which waited for: 3 -> 2; matrix products, arithmetic and copies ran while one was open for 0% -> 0% of each run, Pallas kernels for 3% -> 3%
where the time goes in v4:
time: 101 us
  blocking collectives  60.2 us (60%)
  starting transfers between devices  24.5 us (24%)
  Pallas kernels  8.05 us (8%)
  waiting for transfers between devices  7.11 us (7%)
    all_to_all x3, blocking collectives, spread_out(): lax.all_to_all(array, 'ctx', 0, 0, tiled=True, axis_index_groups=rings)  44.3 us
    ppermute x4, starting transfers between devices, swap(): return lax.ppermute(array, 'ctx', partners)  20.5 us
    all_to_all x1, blocking collectives, per_device(): lax.all_to_all(sums, ('ctx', 'head'), 0, 0, tiled=True, axis_index_groups...  15.9 us
    pallas_call x12, Pallas kernels, call(): pl.pallas_call(body, out_shape=outs if len(outs) > 1 else outs[0], in_spe...  8.05 us
    all_to_all x1, waiting for transfers between devices, spread_out(): lax.all_to_all(array, 'ctx', 0, 0, tiled=True, axis_index_groups=rings)  6.79 us
    all_to_all x1, starting transfers between devices, spread_out(): lax.all_to_all(array, 'ctx', 0, 0, tiled=True, axis_index_groups=rings)  4 us
  transfers between devices with their start and end apart: 5, of which 2 were waited for; matrix products, arithmetic and copies ran while one was open for 0% of the time, Pallas kernels for 3%

profile of v4, /device:TPU:1, one launch (start us, length us, event | category | flops | bytes accessed | tf_op | source)
XLA Modules:
  0.0 100.7 jit_solution(11662763455157074591)
XLA Ops:
  0.6 0.0 copy-start.3
  0.6 2.0 %kv.1 = (f32[32,1280]{1,0:T(8,128)S(1)}, f32[32,1280]{1,0:T(8,128)S(1)}, f32[8,256]{1,0:T(8,128)S(1)}, f32[8,1280]{1,0:T(8,128)S(1)}, bf16[256,640]{1,0:T(8,128)...) custom-call(f32[5]{0:T(128)} %rates.1, ...), custom_call_target="tpu_custom_call" | custom-call | bytes 1310740 | tf_op jit(solution)/shard_map/kv/pallas_call | solution.py:311
  2.7 8.8 %collective-permute-start = (f32[32,1280]{1,0:T(8,128)S(1)}, f32[32,1280]{1,0:T(8,128)S(1)}, u32[]{:S(2)}, u32[]{:S(2)}) collective-permute-start(f32[32,1280]{1,0:T(8,128)S(1)} %get-tuple-element.43), channel_id=1, source_target_pairs={{0,8},{8,0},{16,24},{24,16},{32,40},{40,32},{48,56},{56,48},{64,72... | collective-permute-start | bytes 491528 | tf_op jit(solution)/shard_map/ppermute | solution.py:339
  11.5 0.0 copy-done.3
  11.5 0.7 intra.1
  12.2 0.3 collective-permute-done.got
  12.5 0.1 join.1
  12.5 17.4 %all_to_all.25.totals = f32[32,1,1280]{2,1,0:T(1,128)S(1)} all-to-all(f32[32,1,1280]{2,1,0:T(1,128)S(1)} %join.1), channel_id=1, replica_groups={{0,16,32,48,64,80,96,112,128,144,160,176,192,208,224,240,256,272,288,30..., dimensions={0} | all-to-all | bytes 327680 | tf_op jit(solution)/shard_map/all_to_all | solution.py:342
  29.9 0.3 scan.2
  30.3 3.8 %collective-permute-start.1 = (f32[1280,256]{1,0:T(8,128)S(1)}, f32[1280,256]{1,0:T(8,128)S(1)}, u32[]{:S(2)}, u32[]{:S(2)}) collective-permute-start(f32[1280,256]{1,0:T(8,128)S(1)} %get-tuple-element.55), channel_id=1, source_target_pairs={{0,8},{8,0},{16,24},{24,16},{32,40},{40,32},{48,56},{56,48},{64,72... | collective-permute-start | bytes 3932168 | tf_op jit(solution)/shard_map/ppermute | solution.py:339
  34.1 13.3 %all_to_all.26.prefix = f32[32,1,1280]{2,1,0:T(1,128)S(1)} all-to-all(f32[32,1,1280]{2,1,0:T(1,128)S(1)} %scan.2), channel_id=1, replica_groups={{0,16,32,48,64,80,96,112,128,144,160,176,192,208,224,240,256,272,288,30..., dimensions={0} | all-to-all | bytes 327680 | tf_op jit(solution)/shard_map/all_to_all | solution.py:342
  47.4 0.0 collective-permute-done.1.partner
  47.4 0.3 out.1
  47.7 15.9 %all_to_all.27.sums = f32[16,4,256]{2,1,0:T(4,128)S(1)} all-to-all(f32[16,4,256]{2,1,0:T(4,128)S(1)} %get-tuple-element.56), channel_id=1, replica_groups={{0,1,2,3,4,5,6,7,8,9,10,11,12,13,14,15},{16,17,18,19,20,21,22,23,24,25,..., dimensions={0} | all-to-all | bytes 131072 | tf_op jit(solution)/shard_map/all_to_all | solution.py:365
  63.6 1.1 %grad.1 = (f32[32,1,1280]{2,1,0:T(1,128)}, f32[32,1280]{1,0:T(8,128)S(1)}, bf16[2,320,256]{2,1,0:T(8,128)(2,1)S(1)}) custom-call(f32[8,1280]{1,0:T(8,128)S(1)} %get-tuple-element.41.mixing, f32[16,4,256]{2,1,0:T(4,128)S(1)} %all_to_all.27.sums, f32[2,320,256]{2,1,0:T(8,128)S(1)} %get-tuple-element.57.out, bf16[640,256]{1,0:T(8,128)(2,1)S(1)} %get-tuple-element.52.query_t, ...), custom_call_target="tpu_custom_call" | custom-call | bytes 3055616 | tf_op jit(solution)/shard_map/grad/pallas_call | solution.py:311
  64.7 0.0 copy-start
  64.7 0.0 copy-start.1
  64.7 4.0 %all-to-all-start.3 = ((f32[32,1,1280]{2,1,0:T(1,128)}), f32[32,1,1280]{2,1,0:T(1,128)S(1)}, u32[]{:S(2)}, u32[]{:S(2)}) async-start(f32[32,1,1280]{2,1,0:T(1,128)} %get-tuple-element.59), calls=%async_computation.3 | async-start | bytes 327680 | tf_op jit(solution)/shard_map/all_to_all | solution.py:342
  68.8 2.8 %collective-permute-start.2 = (f32[320,384]{1,0:T(8,128)S(1)}, f32[320,384]{1,0:T(8,128)S(1)}, u32[]{:S(2)}, u32[]{:S(2)}) collective-permute-start(f32[320,384]{1,0:T(8,128)S(1)} %pack.1), channel_id=1, source_target_pairs={{0,8},{8,0},{16,24},{24,16},{32,40},{40,32},{48,56},{56,48},{64,72... | collective-permute-start | bytes 1474568 | tf_op jit(solution)/shard_map/ppermute | solution.py:339
  71.6 6.8 %all-to-all-done.3.totals = f32[32,1,1280]{2,1,0:T(1,128)S(1)} async-done(((f32[32,1,1280]{2,1,0:T(1,128)}), f32[32,1,1280]{2,1,0:T(1,128)S(1)}, u32[]{:S(2)}, u32[]{:S(2)}) %all-to-all-start.3) | async-done | bytes 163872 | tf_op jit(solution)/shard_map/all_to_all | solution.py:342
  78.4 0.3 scan.3
  78.7 0.0 copy-start.2
  78.7 13.6 %all_to_all.28.prefix = f32[32,1,1280]{2,1,0:T(1,128)S(1)} all-to-all(f32[32,1,1280]{2,1,0:T(1,128)S(1)} %scan.3), channel_id=1, replica_groups={{0,16,32,48,64,80,96,112,128,144,160,176,192,208,224,240,256,272,288,30..., dimensions={0} | all-to-all | bytes 327680 | tf_op jit(solution)/shard_map/all_to_all | solution.py:342
  92.3 0.1 spread.1
  92.4 5.1 %collective-permute-start.3 = (f32[32,1280]{1,0:T(8,128)S(1)}, f32[32,1280]{1,0:T(8,128)S(1)}, u32[]{:S(2)}, u32[]{:S(2)}) collective-permute-start(f32[32,1280]{1,0:T(8,128)S(1)} %get-tuple-element.66), channel_id=1, source_target_pairs={{0,8},{8,0},{16,24},{24,16},{32,40},{40,32},{48,56},{56,48},{64,72... | collective-permute-start | bytes 491528 | tf_op jit(solution)/shard_map/ppermute | solution.py:339
  97.5 0.0 collective-permute-done.2.exchange
  97.5 0.0 copy-done
  97.5 0.0 copy-done.1
  97.5 1.5 %local.1 = (bf16[256,640]{1,0:T(8,128)(2,1)}, bf16[5,256,256]{2,1,0:T(8,128)(2,1)S(1)}, bf16[640,256]{1,0:T(8,128)(2,1)S(1)}) custom-call(f32[8,256]{1,0:T(8,128)S(1)} %get-tuple-element.61.rows, f32[8,1280]{1,0:T(8,128)S(1)} %get-tuple-element.41.mixing, bf16[256,640]{1,0:T(8,128)(2,1)S(1)} %copy-done, bf16[256,640]{1,0:T(8,128)(2,1)S(1)} %copy-done.1, ...), custom_call_target="tpu_custom_call" | custom-call | flops 167772160 | bytes 1851392 | tf_op jit(solution)/shard_map/local/pallas_call | solution.py:311
  99.0 0.0 copy-done.2
  99.0 0.5 parts.1
  99.6 0.0 collective-permute-done.3.other
  99.6 1.1 %last.1 = (bf16[256,640]{1,0:T(8,128)(2,1)}, bf16[256,640]{1,0:T(8,128)(2,1)}) custom-call(f32[8,256]{1,0:T(8,128)S(1)} %get-tuple-element.61.rows, f32[8,1280]{1,0:T(8,128)S(1)} %get-tuple-element.41.mixing, bf16[256,640]{1,0:T(8,128)(2,1)S(1)} %copy-done, bf16[256,640]{1,0:T(8,128)(2,1)S(1)} %copy-done.1, f32[32,1280]{1,0:T(8,128)S(1)} %get-tuple-element.65.mine, ...), custom_call_target="tpu_custom_call" | custom-call | bytes 2342912 | tf_op jit(solution)/shard_map/last/pallas_call | solution.py:311
  (2 shorter events, 0.0 us)
Async XLA Ops:
  0.6 10.8 %copy-start.3 = (f32[640]{0:T(1024)S(1)}, f32[640]{0:T(1024)}, u32[]{:S(2)}) copy-start(f32[640]{0:T(1024)} %param.11) | copy-start | bytes 7684
  2.7 9.8 %collective-permute-start = (f32[32,1280]{1,0:T(8,128)S(1)}, f32[32,1280]{1,0:T(8,128)S(1)}, u32[]{:S(2)}, u32[]{:S(2)}) collective-permute-start(f32[32,1280]{1,0:T(8,128)S(1)} %get-tuple-element.43), channel_id=1, source_target_pairs={{0,8},{8,0},{16,24},{24,16},{32,40},{40,32},{48,56},{56,48},{64,72... | collective-permute-start | bytes 491528 | tf_op jit(solution)/shard_map/ppermute | solution.py:339
  30.3 17.2 %collective-permute-start.1 = (f32[1280,256]{1,0:T(8,128)S(1)}, f32[1280,256]{1,0:T(8,128)S(1)}, u32[]{:S(2)}, u32[]{:S(2)}) collective-permute-start(f32[1280,256]{1,0:T(8,128)S(1)} %get-tuple-element.55), channel_id=1, source_target_pairs={{0,8},{8,0},{16,24},{24,16},{32,40},{40,32},{48,56},{56,48},{64,72... | collective-permute-start | bytes 3932168 | tf_op jit(solution)/shard_map/ppermute | solution.py:339
  64.7 32.7 %copy-start = (bf16[256,640]{1,0:T(8,128)(2,1)S(1)}, bf16[256,640]{1,0:T(8,128)(2,1)}, u32[]{:S(2)}) copy-start(bf16[256,640]{1,0:T(8,128)(2,1)} %keys.5) | copy-start | bytes 983044
  64.7 32.8 %copy-start.1 = (bf16[256,640]{1,0:T(8,128)(2,1)S(1)}, bf16[256,640]{1,0:T(8,128)(2,1)}, u32[]{:S(2)}) copy-start(bf16[256,640]{1,0:T(8,128)(2,1)} %values.5) | copy-start | bytes 983044
  64.7 13.6 %all-to-all-start.3 = ((f32[32,1,1280]{2,1,0:T(1,128)}), f32[32,1,1280]{2,1,0:T(1,128)S(1)}, u32[]{:S(2)}, u32[]{:S(2)}) async-start(f32[32,1,1280]{2,1,0:T(1,128)} %get-tuple-element.59), calls=%async_computation.3 | async-start | bytes 327680 | tf_op jit(solution)/shard_map/all_to_all | solution.py:342
  68.8 28.7 %collective-permute-start.2 = (f32[320,384]{1,0:T(8,128)S(1)}, f32[320,384]{1,0:T(8,128)S(1)}, u32[]{:S(2)}, u32[]{:S(2)}) collective-permute-start(f32[320,384]{1,0:T(8,128)S(1)} %pack.1), channel_id=1, source_target_pairs={{0,8},{8,0},{16,24},{24,16},{32,40},{40,32},{48,56},{56,48},{64,72... | collective-permute-start | bytes 1474568 | tf_op jit(solution)/shard_map/ppermute | solution.py:339
  78.7 20.3 %copy-start.2 = (bf16[256,640]{1,0:T(8,128)(2,1)S(1)}, bf16[256,640]{1,0:T(8,128)(2,1)}, u32[]{:S(2)}) copy-start(bf16[256,640]{1,0:T(8,128)(2,1)} %queries.3) | copy-start | bytes 983044
  92.4 7.2 %collective-permute-start.3 = (f32[32,1280]{1,0:T(8,128)S(1)}, f32[32,1280]{1,0:T(8,128)S(1)}, u32[]{:S(2)}, u32[]{:S(2)}) collective-permute-start(f32[32,1280]{1,0:T(8,128)S(1)} %get-tuple-element.66), channel_id=1, source_target_pairs={{0,8},{8,0},{16,24},{24,16},{32,40},{40,32},{48,56},{56,48},{64,72... | collective-permute-start | bytes 491528 | tf_op jit(solution)/shard_map/ppermute | solution.py:339

commit v5 on v4

--- a/solution.py
+++ b/solution.py
@@ -108,13 +108,8 @@
               rate, decays, sems):
     count = rates.shape[0]
     odd = lax.rem(lax.axis_index("ctx"), 2) == 1
-    copies = [pltpu.make_async_copy(rates, rate, sems.at[0])]
-    for h in range(count):
-        for source, target in ((keys, key_in), (values, value_in)):
-            copies.append(pltpu.make_async_copy(
-                source.at[:, lanes_of(h)], target.at[:, lanes_of(h)], sems.at[len(copies)]))
-    for source, target in ((queries, query_in), (out_grad, grad_in)):
-        copies.append(pltpu.make_async_copy(source, target, sems.at[len(copies)]))
+    pairs = ((rates, rate), (keys, key_in), (values, value_in), (queries, query_in), (out_grad, grad_in))
+    copies = [pltpu.make_async_copy(source, target, sems.at[i]) for i, (source, target) in enumerate(pairs)]
     for copy in copies:
         copy.start()
     copies[0].wait()
@@ -130,13 +125,13 @@
         on_second = jnp.where(place == 1, decay, jnp.where(place == 3, 0.0, 1.0))
         mixing[:, h * wide:(h + 1) * wide] = jnp.where(first, on_first, on_second)
         decays[:, lanes_of(h)] = decay_out_of(jnp.full((1, HD), rate[h], F32))
-    for h in range(count):
-        copies[1 + 2 * h].wait()
-        copies[2 + 2 * h].wait()
+    copies[1].wait()
+    copies[2].wait()
+    for h in range(count):
         key_dec = scaled(head(key_in, h), head(decays, h))
         put_halves(keep, send, h, dot(head(value_in, h), key_dec, 0, 0), odd)
-    for copy in copies[1 + 2 * count:]:
-        copy.wait()
+    copies[3].wait()
+    copies[4].wait()
 
 
 def odd_of(mixing, width=HD):
@@ -286,10 +281,11 @@
         value_part[:, lanes_of(h)] = dot(attn[h], whole_grad[rows_of(h, HD), :], 0, 1)
 
 
-def last_kernel(rows, mixing, keys, values, mine, other, key_part, value_part,
-                key_grad, value_grad, key_out, value_out, sems):
+def last_kernel(rows, mixing, keys, values, mine, other, key_part, value_part, query_out,
+                query_grad, key_grad, value_grad, key_out, value_out, sems):
     odd = odd_of(mixing)
-    copies = []
+    copies = [pltpu.make_async_copy(query_out, query_grad, sems.at[2 * (keys.shape[1] // HD)])]
+    copies[0].start()
     for h in range(keys.shape[1] // HD):
         later = get_state(mine, other, h, odd)
         decay_out = decay_out_of(short(rows, h))
@@ -346,7 +342,7 @@
         [half, half, ((8, BLOCK), F32), ((8, lanes), F32)] + [wide16] * 4,
         specs=[HBM] * 5,
         scratch=[pltpu.SMEM((count,), F32), pltpu.VMEM((BLOCK, width), F32),
-                 pltpu.SemaphoreType.DMA((2 * count + 3,))])
+                 pltpu.SemaphoreType.DMA((5,))])
     got = swap(send)
     attn, query_t, intra_t, weighted_t, partner = call(
         intra_kernel, "intra", [rows, mixing, query_in, key_in, value_in, grad_in, gain],
@@ -379,12 +375,13 @@
     key_part, value_part = call(
         parts_kernel, "parts", [queries, attn, back_attn, whole_grad], [wide32, wide32], flops=4 * unit)
     other, key_part, value_part = lax.optimization_barrier((other, key_part, value_part))
-    key_grad, value_grad = call(
-        last_kernel, "last", [rows, mixing, keys, values, mine, other, key_part, value_part], [wide16, wide16],
+    outs = call(
+        last_kernel, "last", [rows, mixing, keys, values, mine, other, key_part, value_part, query_grad],
+        [wide16] * 3,
         scratch=[pltpu.VMEM((BLOCK, width), BF16), pltpu.VMEM((BLOCK, width), BF16),
-                 pltpu.SemaphoreType.DMA((2 * count,))],
+                 pltpu.SemaphoreType.DMA((2 * count + 1,))],
         into=HBM)
-    return query_grad, key_grad, value_grad
+    return tuple(outs)
 
 
 def solution(mesh):

time: 101 us -> 99.8 us (0.988)
  Pallas kernels: 8.05 us -> 6.73 us
    pallas_call x12, Pallas kernels: 8.05 us -> 6.73 us  [call(): pl.pallas_call(body, out_shape=outs if len(outs) > 1 else outs[0], in_spe...]
  transfers between devices with their start and end apart: 5 -> 5, of which waited for: 2 -> 2; matrix products, arithmetic and copies ran while one was open for 0% -> 0% of each run, Pallas kernels for 3% -> 2%
where the time goes in v5:
time: 99.8 us; the launch traced here: 99.4 us
  blocking collectives  60.2 us (60%)
  starting transfers between devices  24.5 us (25%)
  waiting for transfers between devices  7.11 us (7%)
  Pallas kernels  6.73 us (7%)
    all_to_all x3, blocking collectives, spread_out(): lax.all_to_all(array, 'ctx', 0, 0, tiled=True, axis_index_groups=rings)  44.3 us
    ppermute x4, starting transfers between devices, swap(): return lax.ppermute(array, 'ctx', partners)  20.5 us
    all_to_all x1, blocking collectives, per_device(): lax.all_to_all(sums, ('ctx', 'head'), 0, 0, tiled=True, axis_index_groups...  15.9 us
    all_to_all x1, waiting for transfers between devices, spread_out(): lax.all_to_all(array, 'ctx', 0, 0, tiled=True, axis_index_groups=rings)  6.79 us
    pallas_call x12, Pallas kernels, call(): pl.pallas_call(body, out_shape=outs if len(outs) > 1 else outs[0], in_spe...  6.73 us
    all_to_all x1, starting transfers between devices, spread_out(): lax.all_to_all(array, 'ctx', 0, 0, tiled=True, axis_index_groups=rings)  4 us
  transfers between devices with their start and end apart: 5, of which 2 were waited for; matrix products, arithmetic and copies ran while one was open for 0% of the time, Pallas kernels for 2%

profile of v5, /device:TPU:1, one launch (start us, length us, event | category | flops | bytes accessed | tf_op | source)
XLA Modules:
  0.0 99.4 jit_solution(6291729569872071880)
XLA Ops:
  0.6 0.0 copy-start.3
  0.6 1.4 %kv.1 = (f32[32,1280]{1,0:T(8,128)S(1)}, f32[32,1280]{1,0:T(8,128)S(1)}, f32[8,256]{1,0:T(8,128)S(1)}, f32[8,1280]{1,0:T(8,128)S(1)}, bf16[256,640]{1,0:T(8,128)...) custom-call(f32[5]{0:T(128)} %rates.1, ...), custom_call_target="tpu_custom_call" | custom-call | bytes 1310740 | tf_op jit(solution)/shard_map/kv/pallas_call | solution.py:307
  2.1 8.8 %collective-permute-start = (f32[32,1280]{1,0:T(8,128)S(1)}, f32[32,1280]{1,0:T(8,128)S(1)}, u32[]{:S(2)}, u32[]{:S(2)}) collective-permute-start(f32[32,1280]{1,0:T(8,128)S(1)} %get-tuple-element.41), channel_id=1, source_target_pairs={{0,8},{8,0},{16,24},{24,16},{32,40},{40,32},{48,56},{56,48},{64,72... | collective-permute-start | bytes 491528 | tf_op jit(solution)/shard_map/ppermute | solution.py:335
  10.9 0.0 copy-done.3
  10.9 0.7 intra.1
  11.6 0.3 collective-permute-done.got
  11.9 0.1 join.1
  11.9 17.4 %all_to_all.25.totals = f32[32,1,1280]{2,1,0:T(1,128)S(1)} all-to-all(f32[32,1,1280]{2,1,0:T(1,128)S(1)} %join.1), channel_id=1, replica_groups={{0,16,32,48,64,80,96,112,128,144,160,176,192,208,224,240,256,272,288,30..., dimensions={0} | all-to-all | bytes 327680 | tf_op jit(solution)/shard_map/all_to_all | solution.py:338
  29.3 0.3 scan.2
  29.6 3.8 %collective-permute-start.1 = (f32[1280,256]{1,0:T(8,128)S(1)}, f32[1280,256]{1,0:T(8,128)S(1)}, u32[]{:S(2)}, u32[]{:S(2)}) collective-permute-start(f32[1280,256]{1,0:T(8,128)S(1)} %get-tuple-element.53), channel_id=1, source_target_pairs={{0,8},{8,0},{16,24},{24,16},{32,40},{40,32},{48,56},{56,48},{64,72... | collective-permute-start | bytes 3932168 | tf_op jit(solution)/shard_map/ppermute | solution.py:335
  33.5 13.3 %all_to_all.26.prefix = f32[32,1,1280]{2,1,0:T(1,128)S(1)} all-to-all(f32[32,1,1280]{2,1,0:T(1,128)S(1)} %scan.2), channel_id=1, replica_groups={{0,16,32,48,64,80,96,112,128,144,160,176,192,208,224,240,256,272,288,30..., dimensions={0} | all-to-all | bytes 327680 | tf_op jit(solution)/shard_map/all_to_all | solution.py:338
  46.8 0.0 collective-permute-done.1.partner
  46.8 0.3 out.1
  47.1 15.9 %all_to_all.27.sums = f32[16,4,256]{2,1,0:T(4,128)S(1)} all-to-all(f32[16,4,256]{2,1,0:T(4,128)S(1)} %get-tuple-element.54), channel_id=1, replica_groups={{0,1,2,3,4,5,6,7,8,9,10,11,12,13,14,15},{16,17,18,19,20,21,22,23,24,25,..., dimensions={0} | all-to-all | bytes 131072 | tf_op jit(solution)/shard_map/all_to_all | solution.py:361
  63.0 1.1 %grad.1 = (f32[32,1,1280]{2,1,0:T(1,128)}, f32[32,1280]{1,0:T(8,128)S(1)}, bf16[2,320,256]{2,1,0:T(8,128)(2,1)S(1)}) custom-call(f32[8,1280]{1,0:T(8,128)S(1)} %get-tuple-element.39.mixing, f32[16,4,256]{2,1,0:T(4,128)S(1)} %all_to_all.27.sums, f32[2,320,256]{2,1,0:T(8,128)S(1)} %get-tuple-element.55.out, bf16[640,256]{1,0:T(8,128)(2,1)S(1)} %get-tuple-element.50.query_t, ...), custom_call_target="tpu_custom_call" | custom-call | bytes 3055616 | tf_op jit(solution)/shard_map/grad/pallas_call | solution.py:307
  64.1 0.0 copy-start
  64.1 0.0 copy-start.1
  64.1 4.0 %all-to-all-start.3 = ((f32[32,1,1280]{2,1,0:T(1,128)}), f32[32,1,1280]{2,1,0:T(1,128)S(1)}, u32[]{:S(2)}, u32[]{:S(2)}) async-start(f32[32,1,1280]{2,1,0:T(1,128)} %get-tuple-element.57), calls=%async_computation.3 | async-start | bytes 327680 | tf_op jit(solution)/shard_map/all_to_all | solution.py:338
  68.2 2.8 %collective-permute-start.3 = (f32[320,384]{1,0:T(8,128)S(1)}, f32[320,384]{1,0:T(8,128)S(1)}, u32[]{:S(2)}, u32[]{:S(2)}) collective-permute-start(f32[320,384]{1,0:T(8,128)S(1)} %pack.1), channel_id=1, source_target_pairs={{0,8},{8,0},{16,24},{24,16},{32,40},{40,32},{48,56},{56,48},{64,72... | collective-permute-start | bytes 1474568 | tf_op jit(solution)/shard_map/ppermute | solution.py:335
  71.0 6.8 %all-to-all-done.3.totals = f32[32,1,1280]{2,1,0:T(1,128)S(1)} async-done(((f32[32,1,1280]{2,1,0:T(1,128)}), f32[32,1,1280]{2,1,0:T(1,128)S(1)}, u32[]{:S(2)}, u32[]{:S(2)}) %all-to-all-start.3) | async-done | bytes 163872 | tf_op jit(solution)/shard_map/all_to_all | solution.py:338
  77.8 0.3 scan.3
  78.1 0.0 copy-start.2
  78.1 13.6 %all_to_all.28.prefix = f32[32,1,1280]{2,1,0:T(1,128)S(1)} all-to-all(f32[32,1,1280]{2,1,0:T(1,128)S(1)} %scan.3), channel_id=1, replica_groups={{0,16,32,48,64,80,96,112,128,144,160,176,192,208,224,240,256,272,288,30..., dimensions={0} | all-to-all | bytes 327680 | tf_op jit(solution)/shard_map/all_to_all | solution.py:338
  91.7 0.1 spread.1
  91.8 5.1 %collective-permute-start.2 = (f32[32,1280]{1,0:T(8,128)S(1)}, f32[32,1280]{1,0:T(8,128)S(1)}, u32[]{:S(2)}, u32[]{:S(2)}) collective-permute-start(f32[32,1280]{1,0:T(8,128)S(1)} %get-tuple-element.60), channel_id=1, source_target_pairs={{0,8},{8,0},{16,24},{24,16},{32,40},{40,32},{48,56},{56,48},{64,72... | collective-permute-start | bytes 491528 | tf_op jit(solution)/shard_map/ppermute | solution.py:335
  96.9 0.0 collective-permute-done.3.exchange
  96.9 0.0 copy-done
  96.9 0.0 copy-done.1
  96.9 0.8 local.1
  97.7 0.0 copy-done.2
  97.7 0.5 parts.1
  98.3 0.0 collective-permute-done.2.other
  98.3 1.1 %last.1 = (bf16[256,640]{1,0:T(8,128)(2,1)}, bf16[256,640]{1,0:T(8,128)(2,1)}, bf16[256,640]{1,0:T(8,128)(2,1)}) custom-call(f32[8,256]{1,0:T(8,128)S(1)} %get-tuple-element.62.rows, f32[8,1280]{1,0:T(8,128)S(1)} %get-tuple-element.39.mixing, bf16[256,640]{1,0:T(8,128)(2,1)S(1)} %copy-done, bf16[256,640]{1,0:T(8,128)(2,1)S(1)} %copy-done.1, ...), custom_call_target="tpu_custom_call" | custom-call | bytes 2670592 | tf_op jit(solution)/shard_map/last/pallas_call | solution.py:307
  (2 shorter events, 0.0 us)
Async XLA Ops:
  0.6 10.2 %copy-start.3 = (f32[640]{0:T(1024)S(1)}, f32[640]{0:T(1024)}, u32[]{:S(2)}) copy-start(f32[640]{0:T(1024)} %param.11) | copy-start | bytes 7684
  2.1 9.8 %collective-permute-start = (f32[32,1280]{1,0:T(8,128)S(1)}, f32[32,1280]{1,0:T(8,128)S(1)}, u32[]{:S(2)}, u32[]{:S(2)}) collective-permute-start(f32[32,1280]{1,0:T(8,128)S(1)} %get-tuple-element.41), channel_id=1, source_target_pairs={{0,8},{8,0},{16,24},{24,16},{32,40},{40,32},{48,56},{56,48},{64,72... | collective-permute-start | bytes 491528 | tf_op jit(solution)/shard_map/ppermute | solution.py:335
  29.6 17.2 %collective-permute-start.1 = (f32[1280,256]{1,0:T(8,128)S(1)}, f32[1280,256]{1,0:T(8,128)S(1)}, u32[]{:S(2)}, u32[]{:S(2)}) collective-permute-start(f32[1280,256]{1,0:T(8,128)S(1)} %get-tuple-element.53), channel_id=1, source_target_pairs={{0,8},{8,0},{16,24},{24,16},{32,40},{40,32},{48,56},{56,48},{64,72... | collective-permute-start | bytes 3932168 | tf_op jit(solution)/shard_map/ppermute | solution.py:335
  64.1 32.7 %copy-start = (bf16[256,640]{1,0:T(8,128)(2,1)S(1)}, bf16[256,640]{1,0:T(8,128)(2,1)}, u32[]{:S(2)}) copy-start(bf16[256,640]{1,0:T(8,128)(2,1)} %keys.5) | copy-start | bytes 983044
  64.1 32.8 %copy-start.1 = (bf16[256,640]{1,0:T(8,128)(2,1)S(1)}, bf16[256,640]{1,0:T(8,128)(2,1)}, u32[]{:S(2)}) copy-start(bf16[256,640]{1,0:T(8,128)(2,1)} %values.5) | copy-start | bytes 983044
  64.1 13.7 %all-to-all-start.3 = ((f32[32,1,1280]{2,1,0:T(1,128)}), f32[32,1,1280]{2,1,0:T(1,128)S(1)}, u32[]{:S(2)}, u32[]{:S(2)}) async-start(f32[32,1,1280]{2,1,0:T(1,128)} %get-tuple-element.57), calls=%async_computation.3 | async-start | bytes 327680 | tf_op jit(solution)/shard_map/all_to_all | solution.py:338
  68.2 28.7 %collective-permute-start.3 = (f32[320,384]{1,0:T(8,128)S(1)}, f32[320,384]{1,0:T(8,128)S(1)}, u32[]{:S(2)}, u32[]{:S(2)}) collective-permute-start(f32[320,384]{1,0:T(8,128)S(1)} %pack.1), channel_id=1, source_target_pairs={{0,8},{8,0},{16,24},{24,16},{32,40},{40,32},{48,56},{56,48},{64,72... | collective-permute-start | bytes 1474568 | tf_op jit(solution)/shard_map/ppermute | solution.py:335
  78.1 19.6 %copy-start.2 = (bf16[256,640]{1,0:T(8,128)(2,1)S(1)}, bf16[256,640]{1,0:T(8,128)(2,1)}, u32[]{:S(2)}) copy-start(bf16[256,640]{1,0:T(8,128)(2,1)} %queries.3) | copy-start | bytes 983044
  91.8 6.5 %collective-permute-start.2 = (f32[32,1280]{1,0:T(8,128)S(1)}, f32[32,1280]{1,0:T(8,128)S(1)}, u32[]{:S(2)}, u32[]{:S(2)}) collective-permute-start(f32[32,1280]{1,0:T(8,128)S(1)} %get-tuple-element.60), channel_id=1, source_target_pairs={{0,8},{8,0},{16,24},{24,16},{32,40},{40,32},{48,56},{56,48},{64,72... | collective-permute-start | bytes 491528 | tf_op jit(solution)/shard_map/ppermute | solution.py:335

commit v6 on v5

--- a/solution.py
+++ b/solution.py
@@ -349,11 +349,10 @@
         [square, ((width, BLOCK), BF16), rows_half, rows_half, ((2 * width, BLOCK), F32)], flops=4 * unit)
     got, partner = lax.optimization_barrier((got, partner))
     total = call(functools.partial(join_kernel, False), "join", [mixing, keep, got], [flat])
+    total, partner = lax.optimization_barrier((total, partner))
+    partner = swap(partner)
     total = spread_out(total)
-    prefix = call(functools.partial(scan_kernel, False), "scan", [rows, total], [flat])
-    prefix, partner = lax.optimization_barrier((prefix, partner))
-    partner = swap(partner)
-    prefix = spread_out(prefix)
+    prefix = spread_out(call(functools.partial(scan_kernel, False), "scan", [rows, total], [flat]))
     shared = [query_t, intra_t, weighted_t, partner]
     out, held, sums = call(
         out_kernel, "out", [mixing, keep, got, prefix] + shared,

time: 99.8 us -> 99.3 us (level)
  starting transfers between devices: 24.5 us -> 22.9 us
  blocking collectives: 60.2 us -> 61.2 us
    ppermute x4, starting transfers between devices: 20.5 us -> 18.9 us  [swap(): return lax.ppermute(array, 'ctx', partners)]
  transfers between devices with their start and end apart: 5 -> 5, of which waited for: 2 -> 2; matrix products, arithmetic and copies ran while one was open for 0% -> 0% of each run, Pallas kernels for 2% -> 3%
where the time goes in v6:
time: 99.3 us; the launch traced here: 98.8 us
  blocking collectives  61.2 us (62%)
  starting transfers between devices  22.9 us (23%)
  waiting for transfers between devices  7.11 us (7%)
  Pallas kernels  6.73 us (7%)
    all_to_all x3, blocking collectives, spread_out(): lax.all_to_all(array, 'ctx', 0, 0, tiled=True, axis_index_groups=rings)  44.4 us
    ppermute x4, starting transfers between devices, swap(): return lax.ppermute(array, 'ctx', partners)  18.9 us
    all_to_all x1, blocking collectives, per_device(): lax.all_to_all(sums, ('ctx', 'head'), 0, 0, tiled=True, axis_index_groups...  16.8 us
    all_to_all x1, waiting for transfers between devices, spread_out(): lax.all_to_all(array, 'ctx', 0, 0, tiled=True, axis_index_groups=rings)  6.79 us
    pallas_call x12, Pallas kernels, call(): pl.pallas_call(body, out_shape=outs if len(outs) > 1 else outs[0], in_spe...  6.73 us
    all_to_all x1, starting transfers between devices, spread_out(): lax.all_to_all(array, 'ctx', 0, 0, tiled=True, axis_index_groups=rings)  4 us
  transfers between devices with their start and end apart: 5, of which 2 were waited for; matrix products, arithmetic and copies ran while one was open for 0% of the time, Pallas kernels for 3%

profile of v6, /device:TPU:1, one launch (start us, length us, event | category | flops | bytes accessed | tf_op | source)
XLA Modules:
  0.0 98.8 jit_solution(10863001894457486366)
XLA Ops:
  0.6 0.0 copy-start.3
  0.6 1.4 %kv.1 = (f32[32,1280]{1,0:T(8,128)S(1)}, f32[32,1280]{1,0:T(8,128)S(1)}, f32[8,256]{1,0:T(8,128)S(1)}, f32[8,1280]{1,0:T(8,128)S(1)}, bf16[256,640]{1,0:T(8,128)...) custom-call(f32[5]{0:T(128)} %rates.1, ...), custom_call_target="tpu_custom_call" | custom-call | bytes 1310740 | tf_op jit(solution)/shard_map/kv/pallas_call | solution.py:307
  2.1 8.8 %collective-permute-start = (f32[32,1280]{1,0:T(8,128)S(1)}, f32[32,1280]{1,0:T(8,128)S(1)}, u32[]{:S(2)}, u32[]{:S(2)}) collective-permute-start(f32[32,1280]{1,0:T(8,128)S(1)} %get-tuple-element.41), channel_id=1, source_target_pairs={{0,8},{8,0},{16,24},{24,16},{32,40},{40,32},{48,56},{56,48},{64,72... | collective-permute-start | bytes 491528 | tf_op jit(solution)/shard_map/ppermute | solution.py:335
  10.9 0.0 copy-done.3
  10.9 0.7 intra.1
  11.6 0.3 collective-permute-done.got
  11.9 0.1 join.1
  11.9 2.3 %collective-permute-start.1 = (f32[1280,256]{1,0:T(8,128)S(1)}, f32[1280,256]{1,0:T(8,128)S(1)}, u32[]{:S(2)}, u32[]{:S(2)}) collective-permute-start(f32[1280,256]{1,0:T(8,128)S(1)} %get-tuple-element.53), channel_id=1, source_target_pairs={{0,8},{8,0},{16,24},{24,16},{32,40},{40,32},{48,56},{56,48},{64,72... | collective-permute-start | bytes 3932168 | tf_op jit(solution)/shard_map/ppermute | solution.py:335
  14.2 17.6 %all_to_all.25.totals = f32[32,1,1280]{2,1,0:T(1,128)S(1)} all-to-all(f32[32,1,1280]{2,1,0:T(1,128)S(1)} %join.1), channel_id=1, replica_groups={{0,16,32,48,64,80,96,112,128,144,160,176,192,208,224,240,256,272,288,30..., dimensions={0} | all-to-all | bytes 327680 | tf_op jit(solution)/shard_map/all_to_all | solution.py:338
  31.8 0.3 scan.2
  32.1 13.2 %all_to_all.26.prefix = f32[32,1,1280]{2,1,0:T(1,128)S(1)} all-to-all(f32[32,1,1280]{2,1,0:T(1,128)S(1)} %scan.2), channel_id=1, replica_groups={{0,16,32,48,64,80,96,112,128,144,160,176,192,208,224,240,256,272,288,30..., dimensions={0} | all-to-all | bytes 327680 | tf_op jit(solution)/shard_map/all_to_all | solution.py:338
  45.3 0.0 collective-permute-done.1.partner
  45.3 0.3 out.1
  45.6 16.8 %all_to_all.27.sums = f32[16,4,256]{2,1,0:T(4,128)S(1)} all-to-all(f32[16,4,256]{2,1,0:T(4,128)S(1)} %get-tuple-element.54), channel_id=1, replica_groups={{0,1,2,3,4,5,6,7,8,9,10,11,12,13,14,15},{16,17,18,19,20,21,22,23,24,25,..., dimensions={0} | all-to-all | bytes 131072 | tf_op jit(solution)/shard_map/all_to_all | solution.py:360
  62.5 1.1 %grad.1 = (f32[32,1,1280]{2,1,0:T(1,128)}, f32[32,1280]{1,0:T(8,128)S(1)}, bf16[2,320,256]{2,1,0:T(8,128)(2,1)S(1)}) custom-call(f32[8,1280]{1,0:T(8,128)S(1)} %get-tuple-element.39.mixing, f32[16,4,256]{2,1,0:T(4,128)S(1)} %all_to_all.27.sums, f32[2,320,256]{2,1,0:T(8,128)S(1)} %get-tuple-element.55.out, bf16[640,256]{1,0:T(8,128)(2,1)S(1)} %get-tuple-element.50.query_t, ...), custom_call_target="tpu_custom_call" | custom-call | bytes 3055616 | tf_op jit(solution)/shard_map/grad/pallas_call | solution.py:307
  63.6 0.0 copy-start
  63.6 0.0 copy-start.1
  63.6 4.0 %all-to-all-start.3 = ((f32[32,1,1280]{2,1,0:T(1,128)}), f32[32,1,1280]{2,1,0:T(1,128)S(1)}, u32[]{:S(2)}, u32[]{:S(2)}) async-start(f32[32,1,1280]{2,1,0:T(1,128)} %get-tuple-element.57), calls=%async_computation.3 | async-start | bytes 327680 | tf_op jit(solution)/shard_map/all_to_all | solution.py:338
  67.6 2.8 %collective-permute-start.3 = (f32[320,384]{1,0:T(8,128)S(1)}, f32[320,384]{1,0:T(8,128)S(1)}, u32[]{:S(2)}, u32[]{:S(2)}) collective-permute-start(f32[320,384]{1,0:T(8,128)S(1)} %pack.1), channel_id=1, source_target_pairs={{0,8},{8,0},{16,24},{24,16},{32,40},{40,32},{48,56},{56,48},{64,72... | collective-permute-start | bytes 1474568 | tf_op jit(solution)/shard_map/ppermute | solution.py:335
  70.4 6.8 %all-to-all-done.3.totals = f32[32,1,1280]{2,1,0:T(1,128)S(1)} async-done(((f32[32,1,1280]{2,1,0:T(1,128)}), f32[32,1,1280]{2,1,0:T(1,128)S(1)}, u32[]{:S(2)}, u32[]{:S(2)}) %all-to-all-start.3) | async-done | bytes 163872 | tf_op jit(solution)/shard_map/all_to_all | solution.py:338
  77.2 0.3 scan.3
  77.5 0.0 copy-start.2
  77.5 13.6 %all_to_all.28.prefix = f32[32,1,1280]{2,1,0:T(1,128)S(1)} all-to-all(f32[32,1,1280]{2,1,0:T(1,128)S(1)} %scan.3), channel_id=1, replica_groups={{0,16,32,48,64,80,96,112,128,144,160,176,192,208,224,240,256,272,288,30..., dimensions={0} | all-to-all | bytes 327680 | tf_op jit(solution)/shard_map/all_to_all | solution.py:338
  91.1 0.1 spread.1
  91.2 5.1 %collective-permute-start.2 = (f32[32,1280]{1,0:T(8,128)S(1)}, f32[32,1280]{1,0:T(8,128)S(1)}, u32[]{:S(2)}, u32[]{:S(2)}) collective-permute-start(f32[32,1280]{1,0:T(8,128)S(1)} %get-tuple-element.60), channel_id=1, source_target_pairs={{0,8},{8,0},{16,24},{24,16},{32,40},{40,32},{48,56},{56,48},{64,72... | collective-permute-start | bytes 491528 | tf_op jit(solution)/shard_map/ppermute | solution.py:335
  96.3 0.0 collective-permute-done.3.exchange
  96.3 0.0 copy-done
  96.3 0.0 copy-done.1
  96.3 0.8 local.1
  97.1 0.0 copy-done.2
  97.1 0.5 parts.1
  97.7 0.0 collective-permute-done.2.other
  97.7 1.1 %last.1 = (bf16[256,640]{1,0:T(8,128)(2,1)}, bf16[256,640]{1,0:T(8,128)(2,1)}, bf16[256,640]{1,0:T(8,128)(2,1)}) custom-call(f32[8,256]{1,0:T(8,128)S(1)} %get-tuple-element.62.rows, f32[8,1280]{1,0:T(8,128)S(1)} %get-tuple-element.39.mixing, bf16[256,640]{1,0:T(8,128)(2,1)S(1)} %copy-done, bf16[256,640]{1,0:T(8,128)(2,1)S(1)} %copy-done.1, ...), custom_call_target="tpu_custom_call" | custom-call | bytes 2670592 | tf_op jit(solution)/shard_map/last/pallas_call | solution.py:307
  (2 shorter events, 0.0 us)
Async XLA Ops:
  0.6 10.2 %copy-start.3 = (f32[640]{0:T(1024)S(1)}, f32[640]{0:T(1024)}, u32[]{:S(2)}) copy-start(f32[640]{0:T(1024)} %param.11) | copy-start | bytes 7684
  2.1 9.8 %collective-permute-start = (f32[32,1280]{1,0:T(8,128)S(1)}, f32[32,1280]{1,0:T(8,128)S(1)}, u32[]{:S(2)}, u32[]{:S(2)}) collective-permute-start(f32[32,1280]{1,0:T(8,128)S(1)} %get-tuple-element.41), channel_id=1, source_target_pairs={{0,8},{8,0},{16,24},{24,16},{32,40},{40,32},{48,56},{56,48},{64,72... | collective-permute-start | bytes 491528 | tf_op jit(solution)/shard_map/ppermute | solution.py:335
  11.9 33.4 %collective-permute-start.1 = (f32[1280,256]{1,0:T(8,128)S(1)}, f32[1280,256]{1,0:T(8,128)S(1)}, u32[]{:S(2)}, u32[]{:S(2)}) collective-permute-start(f32[1280,256]{1,0:T(8,128)S(1)} %get-tuple-element.53), channel_id=1, source_target_pairs={{0,8},{8,0},{16,24},{24,16},{32,40},{40,32},{48,56},{56,48},{64,72... | collective-permute-start | bytes 3932168 | tf_op jit(solution)/shard_map/ppermute | solution.py:335
  63.6 32.7 %copy-start = (bf16[256,640]{1,0:T(8,128)(2,1)S(1)}, bf16[256,640]{1,0:T(8,128)(2,1)}, u32[]{:S(2)}) copy-start(bf16[256,640]{1,0:T(8,128)(2,1)} %keys.5) | copy-start | bytes 983044
  63.6 32.8 %copy-start.1 = (bf16[256,640]{1,0:T(8,128)(2,1)S(1)}, bf16[256,640]{1,0:T(8,128)(2,1)}, u32[]{:S(2)}) copy-start(bf16[256,640]{1,0:T(8,128)(2,1)} %values.5) | copy-start | bytes 983044
  63.6 13.6 %all-to-all-start.3 = ((f32[32,1,1280]{2,1,0:T(1,128)}), f32[32,1,1280]{2,1,0:T(1,128)S(1)}, u32[]{:S(2)}, u32[]{:S(2)}) async-start(f32[32,1,1280]{2,1,0:T(1,128)} %get-tuple-element.57), calls=%async_computation.3 | async-start | bytes 327680 | tf_op jit(solution)/shard_map/all_to_all | solution.py:338
  67.6 28.7 %collective-permute-start.3 = (f32[320,384]{1,0:T(8,128)S(1)}, f32[320,384]{1,0:T(8,128)S(1)}, u32[]{:S(2)}, u32[]{:S(2)}) collective-permute-start(f32[320,384]{1,0:T(8,128)S(1)} %pack.1), channel_id=1, source_target_pairs={{0,8},{8,0},{16,24},{24,16},{32,40},{40,32},{48,56},{56,48},{64,72... | collective-permute-start | bytes 1474568 | tf_op jit(solution)/shard_map/ppermute | solution.py:335
  77.5 19.6 %copy-start.2 = (bf16[256,640]{1,0:T(8,128)(2,1)S(1)}, bf16[256,640]{1,0:T(8,128)(2,1)}, u32[]{:S(2)}) copy-start(bf16[256,640]{1,0:T(8,128)(2,1)} %queries.3) | copy-start | bytes 983044
  91.2 6.5 %collective-permute-start.2 = (f32[32,1280]{1,0:T(8,128)S(1)}, f32[32,1280]{1,0:T(8,128)S(1)}, u32[]{:S(2)}, u32[]{:S(2)}) collective-permute-start(f32[32,1280]{1,0:T(8,128)S(1)} %get-tuple-element.60), channel_id=1, source_target_pairs={{0,8},{8,0},{16,24},{24,16},{32,40},{40,32},{48,56},{56,48},{64,72... | collective-permute-start | bytes 491528 | tf_op jit(solution)/shard_map/ppermute | solution.py:335

commit v7 on v6

--- a/solution.py
+++ b/solution.py
@@ -126,10 +126,10 @@
         mixing[:, h * wide:(h + 1) * wide] = jnp.where(first, on_first, on_second)
         decays[:, lanes_of(h)] = decay_out_of(jnp.full((1, HD), rate[h], F32))
     copies[1].wait()
+    key_dec = [scaled(head(key_in, h), head(decays, h)) for h in range(count)]
     copies[2].wait()
     for h in range(count):
-        key_dec = scaled(head(key_in, h), head(decays, h))
-        put_halves(keep, send, h, dot(head(value_in, h), key_dec, 0, 0), odd)
+        put_halves(keep, send, h, dot(head(value_in, h), key_dec[h], 0, 0), odd)
     copies[3].wait()
     copies[4].wait()
 

time: 99.3 us -> 99.3 us (level)
  no operation moved by 1% of the time
where the time goes in v7:
time: 99.3 us; the launch traced here: 98.8 us
  blocking collectives  61.2 us (62%)
  starting transfers between devices  22.9 us (23%)
  waiting for transfers between devices  7.11 us (7%)
  Pallas kernels  6.73 us (7%)
    all_to_all x3, blocking collectives, spread_out(): lax.all_to_all(array, 'ctx', 0, 0, tiled=True, axis_index_groups=rings)  44.4 us
    ppermute x4, starting transfers between devices, swap(): return lax.ppermute(array, 'ctx', partners)  18.9 us
    all_to_all x1, blocking collectives, per_device(): lax.all_to_all(sums, ('ctx', 'head'), 0, 0, tiled=True, axis_index_groups...  16.8 us
    all_to_all x1, waiting for transfers between devices, spread_out(): lax.all_to_all(array, 'ctx', 0, 0, tiled=True, axis_index_groups=rings)  6.79 us
    pallas_call x12, Pallas kernels, call(): pl.pallas_call(body, out_shape=outs if len(outs) > 1 else outs[0], in_spe...  6.73 us
    all_to_all x1, starting transfers between devices, spread_out(): lax.all_to_all(array, 'ctx', 0, 0, tiled=True, axis_index_groups=rings)  4 us
  transfers between devices with their start and end apart: 5, of which 2 were waited for; matrix products, arithmetic and copies ran while one was open for 0% of the time, Pallas kernels for 3%

profile of v7, /device:TPU:1, one launch (start us, length us, event | category | flops | bytes accessed | tf_op | source)
XLA Modules:
  0.0 98.8 jit_solution(8741327676705545222)
XLA Ops:
  0.6 0.0 copy-start.3
  0.6 1.4 %kv.1 = (f32[32,1280]{1,0:T(8,128)S(1)}, f32[32,1280]{1,0:T(8,128)S(1)}, f32[8,256]{1,0:T(8,128)S(1)}, f32[8,1280]{1,0:T(8,128)S(1)}, bf16[256,640]{1,0:T(8,128)...) custom-call(f32[5]{0:T(128)} %rates.1, ...), custom_call_target="tpu_custom_call" | custom-call | bytes 1310740 | tf_op jit(solution)/shard_map/kv/pallas_call | solution.py:307
  2.1 8.8 %collective-permute-start = (f32[32,1280]{1,0:T(8,128)S(1)}, f32[32,1280]{1,0:T(8,128)S(1)}, u32[]{:S(2)}, u32[]{:S(2)}) collective-permute-start(f32[32,1280]{1,0:T(8,128)S(1)} %get-tuple-element.41), channel_id=1, source_target_pairs={{0,8},{8,0},{16,24},{24,16},{32,40},{40,32},{48,56},{56,48},{64,72... | collective-permute-start | bytes 491528 | tf_op jit(solution)/shard_map/ppermute | solution.py:335
  10.9 0.0 copy-done.3
  10.9 0.7 intra.1
  11.6 0.3 collective-permute-done.got
  11.9 0.1 join.1
  11.9 2.3 %collective-permute-start.1 = (f32[1280,256]{1,0:T(8,128)S(1)}, f32[1280,256]{1,0:T(8,128)S(1)}, u32[]{:S(2)}, u32[]{:S(2)}) collective-permute-start(f32[1280,256]{1,0:T(8,128)S(1)} %get-tuple-element.53), channel_id=1, source_target_pairs={{0,8},{8,0},{16,24},{24,16},{32,40},{40,32},{48,56},{56,48},{64,72... | collective-permute-start | bytes 3932168 | tf_op jit(solution)/shard_map/ppermute | solution.py:335
  14.2 17.6 %all_to_all.25.totals = f32[32,1,1280]{2,1,0:T(1,128)S(1)} all-to-all(f32[32,1,1280]{2,1,0:T(1,128)S(1)} %join.1), channel_id=1, replica_groups={{0,16,32,48,64,80,96,112,128,144,160,176,192,208,224,240,256,272,288,30..., dimensions={0} | all-to-all | bytes 327680 | tf_op jit(solution)/shard_map/all_to_all | solution.py:338
  31.8 0.3 scan.2
  32.1 13.2 %all_to_all.26.prefix = f32[32,1,1280]{2,1,0:T(1,128)S(1)} all-to-all(f32[32,1,1280]{2,1,0:T(1,128)S(1)} %scan.2), channel_id=1, replica_groups={{0,16,32,48,64,80,96,112,128,144,160,176,192,208,224,240,256,272,288,30..., dimensions={0} | all-to-all | bytes 327680 | tf_op jit(solution)/shard_map/all_to_all | solution.py:338
  45.3 0.0 collective-permute-done.1.partner
  45.3 0.3 out.1
  45.6 16.8 %all_to_all.27.sums = f32[16,4,256]{2,1,0:T(4,128)S(1)} all-to-all(f32[16,4,256]{2,1,0:T(4,128)S(1)} %get-tuple-element.54), channel_id=1, replica_groups={{0,1,2,3,4,5,6,7,8,9,10,11,12,13,14,15},{16,17,18,19,20,21,22,23,24,25,..., dimensions={0} | all-to-all | bytes 131072 | tf_op jit(solution)/shard_map/all_to_all | solution.py:360
  62.5 1.1 %grad.1 = (f32[32,1,1280]{2,1,0:T(1,128)}, f32[32,1280]{1,0:T(8,128)S(1)}, bf16[2,320,256]{2,1,0:T(8,128)(2,1)S(1)}) custom-call(f32[8,1280]{1,0:T(8,128)S(1)} %get-tuple-element.39.mixing, f32[16,4,256]{2,1,0:T(4,128)S(1)} %all_to_all.27.sums, f32[2,320,256]{2,1,0:T(8,128)S(1)} %get-tuple-element.55.out, bf16[640,256]{1,0:T(8,128)(2,1)S(1)} %get-tuple-element.50.query_t, ...), custom_call_target="tpu_custom_call" | custom-call | bytes 3055616 | tf_op jit(solution)/shard_map/grad/pallas_call | solution.py:307
  63.6 0.0 copy-start
  63.6 0.0 copy-start.1
  63.6 4.0 %all-to-all-start.3 = ((f32[32,1,1280]{2,1,0:T(1,128)}), f32[32,1,1280]{2,1,0:T(1,128)S(1)}, u32[]{:S(2)}, u32[]{:S(2)}) async-start(f32[32,1,1280]{2,1,0:T(1,128)} %get-tuple-element.57), calls=%async_computation.3 | async-start | bytes 327680 | tf_op jit(solution)/shard_map/all_to_all | solution.py:338
  67.6 2.8 %collective-permute-start.3 = (f32[320,384]{1,0:T(8,128)S(1)}, f32[320,384]{1,0:T(8,128)S(1)}, u32[]{:S(2)}, u32[]{:S(2)}) collective-permute-start(f32[320,384]{1,0:T(8,128)S(1)} %pack.1), channel_id=1, source_target_pairs={{0,8},{8,0},{16,24},{24,16},{32,40},{40,32},{48,56},{56,48},{64,72... | collective-permute-start | bytes 1474568 | tf_op jit(solution)/shard_map/ppermute | solution.py:335
  70.4 6.8 %all-to-all-done.3.totals = f32[32,1,1280]{2,1,0:T(1,128)S(1)} async-done(((f32[32,1,1280]{2,1,0:T(1,128)}), f32[32,1,1280]{2,1,0:T(1,128)S(1)}, u32[]{:S(2)}, u32[]{:S(2)}) %all-to-all-start.3) | async-done | bytes 163872 | tf_op jit(solution)/shard_map/all_to_all | solution.py:338
  77.2 0.3 scan.3
  77.5 0.0 copy-start.2
  77.5 13.6 %all_to_all.28.prefix = f32[32,1,1280]{2,1,0:T(1,128)S(1)} all-to-all(f32[32,1,1280]{2,1,0:T(1,128)S(1)} %scan.3), channel_id=1, replica_groups={{0,16,32,48,64,80,96,112,128,144,160,176,192,208,224,240,256,272,288,30..., dimensions={0} | all-to-all | bytes 327680 | tf_op jit(solution)/shard_map/all_to_all | solution.py:338
  91.1 0.1 spread.1
  91.2 5.1 %collective-permute-start.2 = (f32[32,1280]{1,0:T(8,128)S(1)}, f32[32,1280]{1,0:T(8,128)S(1)}, u32[]{:S(2)}, u32[]{:S(2)}) collective-permute-start(f32[32,1280]{1,0:T(8,128)S(1)} %get-tuple-element.60), channel_id=1, source_target_pairs={{0,8},{8,0},{16,24},{24,16},{32,40},{40,32},{48,56},{56,48},{64,72... | collective-permute-start | bytes 491528 | tf_op jit(solution)/shard_map/ppermute | solution.py:335
  96.3 0.0 collective-permute-done.3.exchange
  96.3 0.0 copy-done
  96.3 0.0 copy-done.1
  96.3 0.8 local.1
  97.1 0.0 copy-done.2
  97.1 0.6 parts.1
  97.7 0.0 collective-permute-done.2.other
  97.7 1.1 %last.1 = (bf16[256,640]{1,0:T(8,128)(2,1)}, bf16[256,640]{1,0:T(8,128)(2,1)}, bf16[256,640]{1,0:T(8,128)(2,1)}) custom-call(f32[8,256]{1,0:T(8,128)S(1)} %get-tuple-element.62.rows, f32[8,1280]{1,0:T(8,128)S(1)} %get-tuple-element.39.mixing, bf16[256,640]{1,0:T(8,128)(2,1)S(1)} %copy-done, bf16[256,640]{1,0:T(8,128)(2,1)S(1)} %copy-done.1, ...), custom_call_target="tpu_custom_call" | custom-call | bytes 2670592 | tf_op jit(solution)/shard_map/last/pallas_call | solution.py:307
  (2 shorter events, 0.0 us)
Async XLA Ops:
  0.6 10.2 %copy-start.3 = (f32[640]{0:T(1024)S(1)}, f32[640]{0:T(1024)}, u32[]{:S(2)}) copy-start(f32[640]{0:T(1024)} %param.11) | copy-start | bytes 7684
  2.1 9.8 %collective-permute-start = (f32[32,1280]{1,0:T(8,128)S(1)}, f32[32,1280]{1,0:T(8,128)S(1)}, u32[]{:S(2)}, u32[]{:S(2)}) collective-permute-start(f32[32,1280]{1,0:T(8,128)S(1)} %get-tuple-element.41), channel_id=1, source_target_pairs={{0,8},{8,0},{16,24},{24,16},{32,40},{40,32},{48,56},{56,48},{64,72... | collective-permute-start | bytes 491528 | tf_op jit(solution)/shard_map/ppermute | solution.py:335
  11.9 33.4 %collective-permute-start.1 = (f32[1280,256]{1,0:T(8,128)S(1)}, f32[1280,256]{1,0:T(8,128)S(1)}, u32[]{:S(2)}, u32[]{:S(2)}) collective-permute-start(f32[1280,256]{1,0:T(8,128)S(1)} %get-tuple-element.53), channel_id=1, source_target_pairs={{0,8},{8,0},{16,24},{24,16},{32,40},{40,32},{48,56},{56,48},{64,72... | collective-permute-start | bytes 3932168 | tf_op jit(solution)/shard_map/ppermute | solution.py:335
  63.6 32.7 %copy-start = (bf16[256,640]{1,0:T(8,128)(2,1)S(1)}, bf16[256,640]{1,0:T(8,128)(2,1)}, u32[]{:S(2)}) copy-start(bf16[256,640]{1,0:T(8,128)(2,1)} %keys.5) | copy-start | bytes 983044
  63.6 32.8 %copy-start.1 = (bf16[256,640]{1,0:T(8,128)(2,1)S(1)}, bf16[256,640]{1,0:T(8,128)(2,1)}, u32[]{:S(2)}) copy-start(bf16[256,640]{1,0:T(8,128)(2,1)} %values.5) | copy-start | bytes 983044
  63.6 13.6 %all-to-all-start.3 = ((f32[32,1,1280]{2,1,0:T(1,128)}), f32[32,1,1280]{2,1,0:T(1,128)S(1)}, u32[]{:S(2)}, u32[]{:S(2)}) async-start(f32[32,1,1280]{2,1,0:T(1,128)} %get-tuple-element.57), calls=%async_computation.3 | async-start | bytes 327680 | tf_op jit(solution)/shard_map/all_to_all | solution.py:338
  67.6 28.7 %collective-permute-start.3 = (f32[320,384]{1,0:T(8,128)S(1)}, f32[320,384]{1,0:T(8,128)S(1)}, u32[]{:S(2)}, u32[]{:S(2)}) collective-permute-start(f32[320,384]{1,0:T(8,128)S(1)} %pack.1), channel_id=1, source_target_pairs={{0,8},{8,0},{16,24},{24,16},{32,40},{40,32},{48,56},{56,48},{64,72... | collective-permute-start | bytes 1474568 | tf_op jit(solution)/shard_map/ppermute | solution.py:335
  77.5 19.6 %copy-start.2 = (bf16[256,640]{1,0:T(8,128)(2,1)S(1)}, bf16[256,640]{1,0:T(8,128)(2,1)}, u32[]{:S(2)}) copy-start(bf16[256,640]{1,0:T(8,128)(2,1)} %queries.3) | copy-start | bytes 983044
  91.2 6.5 %collective-permute-start.2 = (f32[32,1280]{1,0:T(8,128)S(1)}, f32[32,1280]{1,0:T(8,128)S(1)}, u32[]{:S(2)}, u32[]{:S(2)}) collective-permute-start(f32[32,1280]{1,0:T(8,128)S(1)} %get-tuple-element.60), channel_id=1, source_target_pairs={{0,8},{8,0},{16,24},{24,16},{32,40},{40,32},{48,56},{56,48},{64,72... | collective-permute-start | bytes 491528 | tf_op jit(solution)/shard_map/ppermute | solution.py:335

commit v8 on v7

--- a/solution.py
+++ b/solution.py
@@ -293,9 +293,12 @@
         key_dec = scaled(head(keys, h), decay_out)
         key_out[:, lanes_of(h)] = (head(key_part, h) + dot(value_dec, later, 1, 0)).astype(BF16)
         value_out[:, lanes_of(h)] = (head(value_part, h) + dot(key_dec, later, 1, 1)).astype(BF16)
+        if h % 2 == 0 and h + 1 < keys.shape[1] // HD:
+            continue
+        lanes = slice((h - h % 2) * HD, (h + 1) * HD)
         for which, (source, target) in enumerate(((key_out, key_grad), (value_out, value_grad))):
             copies.append(pltpu.make_async_copy(
-                source.at[:, lanes_of(h)], target.at[:, lanes_of(h)], sems.at[2 * h + which]))
+                source.at[:, lanes], target.at[:, lanes], sems.at[2 * h + which]))
             copies[-1].start()
     for copy in copies:
         copy.wait()

time: 99.3 us -> 99.3 us (level)
  no operation moved by 1% of the time
where the time goes in v8:
time: 99.3 us; the launch traced here: 98.9 us
  blocking collectives  61.2 us (62%)
  starting transfers between devices  22.9 us (23%)
  waiting for transfers between devices  7.11 us (7%)
  Pallas kernels  6.77 us (7%)
    all_to_all x3, blocking collectives, spread_out(): lax.all_to_all(array, 'ctx', 0, 0, tiled=True, axis_index_groups=rings)  44.4 us
    ppermute x4, starting transfers between devices, swap(): return lax.ppermute(array, 'ctx', partners)  18.9 us
    all_to_all x1, blocking collectives, per_device(): lax.all_to_all(sums, ('ctx', 'head'), 0, 0, tiled=True, axis_index_groups...  16.8 us
    all_to_all x1, waiting for transfers between devices, spread_out(): lax.all_to_all(array, 'ctx', 0, 0, tiled=True, axis_index_groups=rings)  6.79 us
    pallas_call x12, Pallas kernels, call(): pl.pallas_call(body, out_shape=outs if len(outs) > 1 else outs[0], in_spe...  6.77 us
    all_to_all x1, starting transfers between devices, spread_out(): lax.all_to_all(array, 'ctx', 0, 0, tiled=True, axis_index_groups=rings)  4 us
  transfers between devices with their start and end apart: 5, of which 2 were waited for; matrix products, arithmetic and copies ran while one was open for 0% of the time, Pallas kernels for 3%

profile of v8, /device:TPU:1, one launch (start us, length us, event | category | flops | bytes accessed | tf_op | source)
XLA Modules:
  0.0 98.9 jit_solution(15315552427904919643)
XLA Ops:
  0.6 0.0 copy-start.3
  0.6 1.4 %kv.1 = (f32[32,1280]{1,0:T(8,128)S(1)}, f32[32,1280]{1,0:T(8,128)S(1)}, f32[8,256]{1,0:T(8,128)S(1)}, f32[8,1280]{1,0:T(8,128)S(1)}, bf16[256,640]{1,0:T(8,128)...) custom-call(f32[5]{0:T(128)} %rates.1, ...), custom_call_target="tpu_custom_call" | custom-call | bytes 1310740 | tf_op jit(solution)/shard_map/kv/pallas_call | solution.py:310
  2.1 8.8 %collective-permute-start = (f32[32,1280]{1,0:T(8,128)S(1)}, f32[32,1280]{1,0:T(8,128)S(1)}, u32[]{:S(2)}, u32[]{:S(2)}) collective-permute-start(f32[32,1280]{1,0:T(8,128)S(1)} %get-tuple-element.41), channel_id=1, source_target_pairs={{0,8},{8,0},{16,24},{24,16},{32,40},{40,32},{48,56},{56,48},{64,72... | collective-permute-start | bytes 491528 | tf_op jit(solution)/shard_map/ppermute | solution.py:338
  10.9 0.0 copy-done.3
  10.9 0.7 intra.1
  11.6 0.3 collective-permute-done.got
  11.9 0.1 join.1
  11.9 2.3 %collective-permute-start.1 = (f32[1280,256]{1,0:T(8,128)S(1)}, f32[1280,256]{1,0:T(8,128)S(1)}, u32[]{:S(2)}, u32[]{:S(2)}) collective-permute-start(f32[1280,256]{1,0:T(8,128)S(1)} %get-tuple-element.53), channel_id=1, source_target_pairs={{0,8},{8,0},{16,24},{24,16},{32,40},{40,32},{48,56},{56,48},{64,72... | collective-permute-start | bytes 3932168 | tf_op jit(solution)/shard_map/ppermute | solution.py:338
  14.2 17.6 %all_to_all.25.totals = f32[32,1,1280]{2,1,0:T(1,128)S(1)} all-to-all(f32[32,1,1280]{2,1,0:T(1,128)S(1)} %join.1), channel_id=1, replica_groups={{0,16,32,48,64,80,96,112,128,144,160,176,192,208,224,240,256,272,288,30..., dimensions={0} | all-to-all | bytes 327680 | tf_op jit(solution)/shard_map/all_to_all | solution.py:341
  31.8 0.3 scan.2
  32.1 13.2 %all_to_all.26.prefix = f32[32,1,1280]{2,1,0:T(1,128)S(1)} all-to-all(f32[32,1,1280]{2,1,0:T(1,128)S(1)} %scan.2), channel_id=1, replica_groups={{0,16,32,48,64,80,96,112,128,144,160,176,192,208,224,240,256,272,288,30..., dimensions={0} | all-to-all | bytes 327680 | tf_op jit(solution)/shard_map/all_to_all | solution.py:341
  45.3 0.0 collective-permute-done.1.partner
  45.3 0.3 out.1
  45.6 16.8 %all_to_all.27.sums = f32[16,4,256]{2,1,0:T(4,128)S(1)} all-to-all(f32[16,4,256]{2,1,0:T(4,128)S(1)} %get-tuple-element.54), channel_id=1, replica_groups={{0,1,2,3,4,5,6,7,8,9,10,11,12,13,14,15},{16,17,18,19,20,21,22,23,24,25,..., dimensions={0} | all-to-all | bytes 131072 | tf_op jit(solution)/shard_map/all_to_all | solution.py:363
  62.5 1.1 %grad.1 = (f32[32,1,1280]{2,1,0:T(1,128)}, f32[32,1280]{1,0:T(8,128)S(1)}, bf16[2,320,256]{2,1,0:T(8,128)(2,1)S(1)}) custom-call(f32[8,1280]{1,0:T(8,128)S(1)} %get-tuple-element.39.mixing, f32[16,4,256]{2,1,0:T(4,128)S(1)} %all_to_all.27.sums, f32[2,320,256]{2,1,0:T(8,128)S(1)} %get-tuple-element.55.out, bf16[640,256]{1,0:T(8,128)(2,1)S(1)} %get-tuple-element.50.query_t, ...), custom_call_target="tpu_custom_call" | custom-call | bytes 3055616 | tf_op jit(solution)/shard_map/grad/pallas_call | solution.py:310
  63.6 0.0 copy-start
  63.6 0.0 copy-start.1
  63.6 4.0 %all-to-all-start.3 = ((f32[32,1,1280]{2,1,0:T(1,128)}), f32[32,1,1280]{2,1,0:T(1,128)S(1)}, u32[]{:S(2)}, u32[]{:S(2)}) async-start(f32[32,1,1280]{2,1,0:T(1,128)} %get-tuple-element.57), calls=%async_computation.3 | async-start | bytes 327680 | tf_op jit(solution)/shard_map/all_to_all | solution.py:341
  67.6 2.8 %collective-permute-start.3 = (f32[320,384]{1,0:T(8,128)S(1)}, f32[320,384]{1,0:T(8,128)S(1)}, u32[]{:S(2)}, u32[]{:S(2)}) collective-permute-start(f32[320,384]{1,0:T(8,128)S(1)} %pack.1), channel_id=1, source_target_pairs={{0,8},{8,0},{16,24},{24,16},{32,40},{40,32},{48,56},{56,48},{64,72... | collective-permute-start | bytes 1474568 | tf_op jit(solution)/shard_map/ppermute | solution.py:338
  70.4 6.8 %all-to-all-done.3.totals = f32[32,1,1280]{2,1,0:T(1,128)S(1)} async-done(((f32[32,1,1280]{2,1,0:T(1,128)}), f32[32,1,1280]{2,1,0:T(1,128)S(1)}, u32[]{:S(2)}, u32[]{:S(2)}) %all-to-all-start.3) | async-done | bytes 163872 | tf_op jit(solution)/shard_map/all_to_all | solution.py:341
  77.2 0.3 scan.3
  77.5 0.0 copy-start.2
  77.5 13.6 %all_to_all.28.prefix = f32[32,1,1280]{2,1,0:T(1,128)S(1)} all-to-all(f32[32,1,1280]{2,1,0:T(1,128)S(1)} %scan.3), channel_id=1, replica_groups={{0,16,32,48,64,80,96,112,128,144,160,176,192,208,224,240,256,272,288,30..., dimensions={0} | all-to-all | bytes 327680 | tf_op jit(solution)/shard_map/all_to_all | solution.py:341
  91.1 0.1 spread.1
  91.2 5.1 %collective-permute-start.2 = (f32[32,1280]{1,0:T(8,128)S(1)}, f32[32,1280]{1,0:T(8,128)S(1)}, u32[]{:S(2)}, u32[]{:S(2)}) collective-permute-start(f32[32,1280]{1,0:T(8,128)S(1)} %get-tuple-element.60), channel_id=1, source_target_pairs={{0,8},{8,0},{16,24},{24,16},{32,40},{40,32},{48,56},{56,48},{64,72... | collective-permute-start | bytes 491528 | tf_op jit(solution)/shard_map/ppermute | solution.py:338
  96.3 0.0 collective-permute-done.3.exchange
  96.3 0.0 copy-done
  96.3 0.0 copy-done.1
  96.3 0.8 local.1
  97.1 0.0 copy-done.2
  97.1 0.6 parts.1
  97.7 0.0 collective-permute-done.2.other
  97.7 1.2 %last.1 = (bf16[256,640]{1,0:T(8,128)(2,1)}, bf16[256,640]{1,0:T(8,128)(2,1)}, bf16[256,640]{1,0:T(8,128)(2,1)}) custom-call(f32[8,256]{1,0:T(8,128)S(1)} %get-tuple-element.62.rows, f32[8,1280]{1,0:T(8,128)S(1)} %get-tuple-element.39.mixing, bf16[256,640]{1,0:T(8,128)(2,1)S(1)} %copy-done, bf16[256,640]{1,0:T(8,128)(2,1)S(1)} %copy-done.1, ...), custom_call_target="tpu_custom_call" | custom-call | bytes 2670592 | tf_op jit(solution)/shard_map/last/pallas_call | solution.py:310
  (2 shorter events, 0.0 us)
Async XLA Ops:
  0.6 10.2 %copy-start.3 = (f32[640]{0:T(1024)S(1)}, f32[640]{0:T(1024)}, u32[]{:S(2)}) copy-start(f32[640]{0:T(1024)} %param.11) | copy-start | bytes 7684
  2.1 9.8 %collective-permute-start = (f32[32,1280]{1,0:T(8,128)S(1)}, f32[32,1280]{1,0:T(8,128)S(1)}, u32[]{:S(2)}, u32[]{:S(2)}) collective-permute-start(f32[32,1280]{1,0:T(8,128)S(1)} %get-tuple-element.41), channel_id=1, source_target_pairs={{0,8},{8,0},{16,24},{24,16},{32,40},{40,32},{48,56},{56,48},{64,72... | collective-permute-start | bytes 491528 | tf_op jit(solution)/shard_map/ppermute | solution.py:338
  11.9 33.4 %collective-permute-start.1 = (f32[1280,256]{1,0:T(8,128)S(1)}, f32[1280,256]{1,0:T(8,128)S(1)}, u32[]{:S(2)}, u32[]{:S(2)}) collective-permute-start(f32[1280,256]{1,0:T(8,128)S(1)} %get-tuple-element.53), channel_id=1, source_target_pairs={{0,8},{8,0},{16,24},{24,16},{32,40},{40,32},{48,56},{56,48},{64,72... | collective-permute-start | bytes 3932168 | tf_op jit(solution)/shard_map/ppermute | solution.py:338
  63.6 32.7 %copy-start = (bf16[256,640]{1,0:T(8,128)(2,1)S(1)}, bf16[256,640]{1,0:T(8,128)(2,1)}, u32[]{:S(2)}) copy-start(bf16[256,640]{1,0:T(8,128)(2,1)} %keys.5) | copy-start | bytes 983044
  63.6 32.8 %copy-start.1 = (bf16[256,640]{1,0:T(8,128)(2,1)S(1)}, bf16[256,640]{1,0:T(8,128)(2,1)}, u32[]{:S(2)}) copy-start(bf16[256,640]{1,0:T(8,128)(2,1)} %values.5) | copy-start | bytes 983044
  63.6 13.6 %all-to-all-start.3 = ((f32[32,1,1280]{2,1,0:T(1,128)}), f32[32,1,1280]{2,1,0:T(1,128)S(1)}, u32[]{:S(2)}, u32[]{:S(2)}) async-start(f32[32,1,1280]{2,1,0:T(1,128)} %get-tuple-element.57), calls=%async_computation.3 | async-start | bytes 327680 | tf_op jit(solution)/shard_map/all_to_all | solution.py:341
  67.6 28.7 %collective-permute-start.3 = (f32[320,384]{1,0:T(8,128)S(1)}, f32[320,384]{1,0:T(8,128)S(1)}, u32[]{:S(2)}, u32[]{:S(2)}) collective-permute-start(f32[320,384]{1,0:T(8,128)S(1)} %pack.1), channel_id=1, source_target_pairs={{0,8},{8,0},{16,24},{24,16},{32,40},{40,32},{48,56},{56,48},{64,72... | collective-permute-start | bytes 1474568 | tf_op jit(solution)/shard_map/ppermute | solution.py:338
  77.5 19.6 %copy-start.2 = (bf16[256,640]{1,0:T(8,128)(2,1)S(1)}, bf16[256,640]{1,0:T(8,128)(2,1)}, u32[]{:S(2)}) copy-start(bf16[256,640]{1,0:T(8,128)(2,1)} %queries.3) | copy-start | bytes 983044
  91.2 6.5 %collective-permute-start.2 = (f32[32,1280]{1,0:T(8,128)S(1)}, f32[32,1280]{1,0:T(8,128)S(1)}, u32[]{:S(2)}, u32[]{:S(2)}) collective-permute-start(f32[32,1280]{1,0:T(8,128)S(1)} %get-tuple-element.60), channel_id=1, source_target_pairs={{0,8},{8,0},{16,24},{24,16},{32,40},{40,32},{48,56},{56,48},{64,72... | collective-permute-start | bytes 491528 | tf_op jit(solution)/shard_map/ppermute | solution.py:338
